TPU v7x, 32 devices: a whole 2x2x4 slice. The times are simulated.
32 devices in a mesh: seq: 8 (over z, x), dp: 4 (over y, core).
Axes of the slice: x: 2, y: 2, z: 4, core: 2. Of those that a mesh axis runs over, the one named last changes fastest.
Arguments:
- signal: bfloat16 [4, 4096, 768], P('dp', 'seq'), may hold values from -6 to 6
- first_kernel: bfloat16 [3, 768, 768], replicated, may hold values from -0.125 to 0.125
- second_kernel: bfloat16 [3, 768, 768], replicated, may hold values from -0.125 to 0.125
- cotangent: bfloat16 [4, 4096, 768], P('dp', 'seq'), may hold values from -6 to 6
Outputs:
- output: bfloat16 [4, 4096, 768], P('dp', 'seq')
- grad_signal: bfloat16 [4, 4096, 768], P('dp', 'seq')
- first_kernel_gradient: float32 [3, 768, 768], P(None, 'seq')
- second_kernel_gradient: float32 [3, 768, 768], P(None, 'seq')
All inputs are finite; a program needn't handle non-finite values.
Results may differ from a plain program's by a relative error of at most 0.01.
Values may be sent and summed in bfloat16 or wider, within the bound.
A program may use at most 128 MiB of HBM per device.

v0:
```python
import math

import jax
import jax.numpy as jnp
from jax import lax
from jax.sharding import PartitionSpec as P

FIRST_DILATION = 64
SECOND_DILATION = 128


def padded(block, sides, width):
    for axis, dim in sides:
        count = lax.axis_size(axis)
        forward = [(i, i + 1) for i in range(count - 1)]
        backward = [(target, source) for source, target in forward]
        low = lax.ppermute(
            lax.slice_in_dim(block, block.shape[dim] - width, None, axis=dim), axis, forward
        )
        high = lax.ppermute(lax.slice_in_dim(block, 0, width, axis=dim), axis, backward)
        block = jnp.concatenate([low, block, high], axis=dim)
    return block


def gelu_tanh(v):
    return jax.nn.gelu(v, approximate=True)


def convolve_forward(padded_input, kernel_weight, dilation_step, element_count):
    total_sum = jnp.einsum(
        "wlc,cd->wld",
        padded_input[:, 0:element_count],
        kernel_weight[0],
        preferred_element_type=jnp.float32,
    )
    for tap_index in range(1, 3):
        total_sum = total_sum + jnp.einsum(
            "wlc,cd->wld",
            padded_input[:, tap_index * dilation_step : tap_index * dilation_step + element_count],
            kernel_weight[tap_index],
            preferred_element_type=jnp.float32,
        )
    return total_sum


def convolve_backward(gradient_padded, kernel_weight, dilation_step, element_count):
    total_sum = jnp.einsum(
        "wld,cd->wlc",
        gradient_padded[:, 2 * dilation_step : 2 * dilation_step + element_count],
        kernel_weight[0],
        preferred_element_type=jnp.float32,
    )
    for tap_index in range(1, 3):
        total_sum = total_sum + jnp.einsum(
            "wld,cd->wlc",
            gradient_padded[
                :, (2 - tap_index) * dilation_step : (2 - tap_index) * dilation_step + element_count
            ],
            kernel_weight[tap_index],
            preferred_element_type=jnp.float32,
        )
    return total_sum


def kernel_pieces(activation_padded, gradient_value, dilation_step, element_count, scale_factor):
    return (
        jnp.stack(
            [
                jnp.einsum(
                    "wlc,wld->cd",
                    activation_padded[
                        :, tap_index * dilation_step : tap_index * dilation_step + element_count
                    ],
                    gradient_value,
                    preferred_element_type=jnp.float32,
                )
                for tap_index in range(3)
            ]
        )
        * scale_factor
    )


def borders_forward(receptive_field, dilation_step):
    return padded(receptive_field, (("seq", 1),), dilation_step)


def borders_backward(receptive_field, dilation_step):
    return padded(receptive_field, (("seq", 1),), dilation_step)


def kernel_reduction(terms):
    share = lax.psum_scatter(terms, "seq", scatter_dimension=1, tiled=True)
    return lax.psum(share, "dp")


def per_device(signal, first_kernel, second_kernel, cotangent):
    element_count = signal.shape[1]
    n_seq = lax.axis_size("seq")
    tokens_all = signal.shape[0] * lax.axis_size("dp") * element_count * n_seq
    scale_factor = 1.0 / math.sqrt(tokens_all)
    signal_float = signal.astype(jnp.float32)
    first_activation = gelu_tanh(signal_float).astype(jnp.bfloat16)
    first_margin = borders_forward(first_activation, FIRST_DILATION)
    hidden_state = (
        signal_float + convolve_forward(first_margin, first_kernel, FIRST_DILATION, element_count)
    ).astype(jnp.bfloat16)
    middle_float = hidden_state.astype(jnp.float32)
    second_activation = gelu_tanh(middle_float).astype(jnp.bfloat16)
    second_margin = borders_forward(second_activation, SECOND_DILATION)
    output = (
        middle_float
        + convolve_forward(second_margin, second_kernel, SECOND_DILATION, element_count)
    ).astype(jnp.bfloat16)
    upstream_padded = borders_backward(cotangent, SECOND_DILATION)
    second_backward = convolve_backward(
        upstream_padded, second_kernel, SECOND_DILATION, element_count
    )
    _, pull_b = jax.vjp(gelu_tanh, middle_float)
    middle_gradient = (cotangent.astype(jnp.float32) + pull_b(second_backward)[0]).astype(
        jnp.bfloat16
    )
    second_kernel_gradient = kernel_reduction(
        kernel_pieces(second_margin, cotangent, SECOND_DILATION, element_count, scale_factor)
    )
    middle_padded = borders_backward(middle_gradient, FIRST_DILATION)
    first_backward = convolve_backward(middle_padded, first_kernel, FIRST_DILATION, element_count)
    _, pull_a = jax.vjp(gelu_tanh, signal_float)
    grad_signal = (middle_gradient.astype(jnp.float32) + pull_a(first_backward)[0]).astype(
        jnp.bfloat16
    )
    first_kernel_gradient = kernel_reduction(
        kernel_pieces(first_margin, middle_gradient, FIRST_DILATION, element_count, scale_factor)
    )
    return (output, grad_signal, first_kernel_gradient, second_kernel_gradient)


def solution(mesh):
    placed = (P("dp", "seq", None), P(), P(), P("dp", "seq", None))
    return jax.shard_map(
        per_device,
        mesh=mesh,
        in_specs=placed,
        out_specs=(
            P("dp", "seq", None),
            P("dp", "seq", None),
            P(None, "seq", None),
            P(None, "seq", None),
        ),
        check_vma=False,
    )
```

profile of v0, /device:TPU:0, one launch (start us, length us, event | category | flops | bytes accessed | tf_op | source)
XLA Modules:
  0.0 362.7 jit_solution(4751100304364982654)
XLA Ops:
  7.2 0.0 copy-start.2
  7.2 0.0 reduce-scatter.3.cloned.1.call-start
  7.2 1.1 fusion.123
  8.3 4.9 %collective-permute-start.5 = (bf16[1,128,768]{2,1,0:T(8,128)(2,1)S(1)}, bf16[1,128,768]{2,1,0:T(8,128)(2,1)S(1)}, u32[]{:S(2)}, u32[]{:S(2)}) collective-permute-start(bf16[1,128,768]{2,1,0:T(8,128)(2,1)S(1)} %get-tuple-element.8), channel_id=1, source_target_pairs={{0,4},{4,8},{8,12},{12,16},{16,20},{20,24},{24,28},{1,5},{5,9},{9,... | collective-permute-start | bytes 589832 | tf_op jit(solution)/shard_map/ppermute | solution.py:17
  13.2 1.3 collective-permute-start.4
  14.5 1.7 fusion.13
  16.2 1.3 collective-permute-start.1
  17.5 0.0 copy-start
  17.5 0.0 copy-start.6
  17.5 5.4 %collective-permute-start = (bf16[1,64,768]{2,1,0:T(8,128)(2,1)S(1)}, bf16[1,64,768]{2,1,0:T(8,128)(2,1)S(1)}, u32[]{:S(2)}, u32[]{:S(2)}) collective-permute-start(bf16[1,64,768]{2,1,0:T(8,128)(2,1)S(1)} %get-tuple-element.13), channel_id=1, source_target_pairs={{0,4},{4,8},{8,12},{12,16},{16,20},{20,24},{24,28},{1,5},{5,9},{9,... | collective-permute-start | bytes 294920 | tf_op jit(solution)/shard_map/ppermute | solution.py:17
  23.0 0.0 copy-done.2
  23.0 2.4 fusion.52
  25.4 0.0 copy-done
  25.4 0.0 copy-done.6
  25.4 0.0 copy-start.7
  25.4 0.8 fusion.34
  26.2 0.0 collective-permute-done
  26.2 1.2 copy-done.7
  27.4 0.8 fusion.56
  28.2 0.0 collective-permute-done.1
  28.2 1.3 fusion.20
  29.5 0.0 copy-start.4
  29.5 0.0 collective-permute-done.4
  29.5 0.8 fusion.38
  30.3 0.0 collective-permute-done.5
  30.3 0.0 copy-done.4
  30.3 1.8 fusion.5
  32.1 1.0 convolution_bitcast_fusion.4
  33.2 0.8 convolution_bitcast_fusion.3
  34.0 0.8 convolution_bitcast_fusion.5
  34.8 3.1 maximum_multiply_fusion
  37.9 0.0 reduce-scatter.3.cloned.1.call-update
  37.9 0.0 reduce-scatter.5.cloned.1.call-start
  38.0 1.4 collective-permute-start.3
  39.4 5.6 %collective-permute-start.2 = (bf16[1,128,768]{2,1,0:T(8,128)(2,1)S(1)}, bf16[1,128,768]{2,1,0:T(8,128)(2,1)S(1)}, u32[]{:S(2)}, u32[]{:S(2)}) collective-permute-start(bf16[1,128,768]{2,1,0:T(8,128)(2,1)S(1)} %get-tuple-element.11), channel_id=1, source_target_pairs={{0,4},{4,8},{8,12},{12,16},{16,20},{20,24},{24,28},{1,5},{5,9},{9,... | collective-permute-start | bytes 589832 | tf_op jit(solution)/shard_map/ppermute | solution.py:17
  45.1 0.0 copy-done.5
  45.1 1.1 convolution_bitcast_fusion.1
  46.1 0.6 collective-permute-done.3
  46.7 0.8 convolution_bitcast_fusion
  47.5 7.8 %collective-permute-done.2 = bf16[1,128,768]{2,1,0:T(8,128)(2,1)S(1)} collective-permute-done((bf16[1,128,768]{2,1,0:T(8,128)(2,1)S(1)}, bf16[1,128,768]{2,1,0:T(8,128)(2,1)S(1)}, u32[]{:S(2)}, u32[]{:S(2)}) %collective-permute-start.2) | collective-permute-done | bytes 196640 | tf_op jit(solution)/shard_map/ppermute | solution.py:17
  55.3 0.8 convolution_bitcast_fusion.2
  56.1 3.1 maximum_multiply_fusion.1
  59.2 0.0 reduce-scatter.5.cloned.1.call-update
  59.3 0.0 all-reduce.3.cloned.1.call-start
  59.3 2.6 fusion.36
  61.9 0.7 fusion.122
  62.6 5.0 %collective-permute-start.7 = (bf16[1,64,768]{2,1,0:T(8,128)(2,1)}, bf16[1,64,768]{2,1,0:T(8,128)(2,1)}, u32[]{:S(2)}, u32[]{:S(2)}) collective-permute-start(bf16[1,64,768]{2,1,0:T(8,128)(2,1)} %get-tuple-element.6), channel_id=1, source_target_pairs={{0,4},{4,8},{8,12},{12,16},{16,20},{20,24},{24,28},{1,5},{5,9},{9,... | collective-permute-start | bytes 294920 | tf_op jit(solution)/shard_map/ppermute | solution.py:17
  67.7 1.3 collective-permute-start.6
  69.0 3.3 fusion.50
  72.2 3.3 fusion.40
  75.5 97.5 %reduce-scatter.3.cloned.1.call-done = f32[3,96,768]{2,1,0:T(8,128)} async-done(((f32[3,768,768]{2,1,0:T(8,128)}), f32[3,96,768]{2,1,0:T(8,128)}) %reduce-scatter.3.cloned.1.call-update) | async-done | bytes 884752 | tf_op jit(solution)/shard_map/reduce_scatter | solution.py:93
  173.0 132.3 %reduce-scatter.5.cloned.1.call-done = f32[3,96,768]{2,1,0:T(8,128)} async-done(((f32[3,768,768]{2,1,0:T(8,128)}), f32[3,96,768]{2,1,0:T(8,128)}) %reduce-scatter.5.cloned.1.call-update) | async-done | bytes 884752 | tf_op jit(solution)/shard_map/reduce_scatter | solution.py:93
  305.3 0.0 all-reduce.3.cloned.1.call-update
  305.3 0.0 copy-start.8
  305.3 3.8 %fusion.21 = bf16[1,512,768]{2,1,0:T(8,128)(2,1)} fusion(bf16[1,512,768]{2,1,0:T(8,128)(2,1)} %copy-done.4, f32[512,768]{1,0:T(8,128)} %fusion.40, f32[512,768]{1,0:T(8,128)S(1)} %fusion.36, bf16[3,768,768]{2,1,0:T(8,128)(2,1)} %param.6, bf16[1,128,768]{2,1,0:T(8,128)(2,1)S(1)} %collective-permute-done.3, bf16[1,512,768]{2,1,0:T(8,128)(2,1)S(1)} %get-tuple-element.14), kind=kOutput, calls=%fused_computation.41 | convolution fusion | flops 607518720 | bytes 6881280 | tf_op jit(solution)/shard_map/wlc,cd->wld/dot_general | solution.py:37
  309.1 0.0 collective-permute-done.6
  309.1 0.0 copy-done.8
  309.1 1.9 fusion.54
  311.0 0.0 collective-permute-done.7
  311.0 3.5 fusion.9
  314.6 38.4 %all-reduce.3.cloned.1.call-done = (f32[3,96,768]{2,1,0:T(8,128)}, f32[3,96,768]{2,1,0:T(8,128)}) async-done(((f32[3,96,768]{2,1,0:T(8,128)}, f32[3,96,768]{2,1,0:T(8,128)}), (f32[3,96,768]{2,1,0:T(8,128)}, f32[3,96,768]{2,1,0:T(8,128)})) %all-reduce.3.cloned.1.call-update) | async-done | bytes 1769488 | tf_op jit(solution)/shard_map/psum | solution.py:94
  353.0 2.2 copy.10
  355.2 0.0 copy-done.1
  355.2 0.9 copy.11
  (8 shorter events, 0.1 us)
Async XLA Ops:
  7.2 15.8 %copy-start.2 = (bf16[1,512,768]{2,1,0:T(8,128)(2,1)S(1)}, bf16[1,512,768]{2,1,0:T(8,128)(2,1)}, u32[]{:S(2)}) copy-start(bf16[1,512,768]{2,1,0:T(8,128)(2,1)} %param.4) | copy-start | bytes 2359300
  7.2 165.8 %reduce-scatter.3.cloned.1.call-start = ((), (), s32[]{:S(2)}) async-start(), calls=%async_computation.2 | async-start | bytes 7962624 | tf_op jit(solution)/shard_map/reduce_scatter | solution.py:93
  8.3 22.0 %collective-permute-start.5 = (bf16[1,128,768]{2,1,0:T(8,128)(2,1)S(1)}, bf16[1,128,768]{2,1,0:T(8,128)(2,1)S(1)}, u32[]{:S(2)}, u32[]{:S(2)}) collective-permute-start(bf16[1,128,768]{2,1,0:T(8,128)(2,1)S(1)} %get-tuple-element.8), channel_id=1, source_target_pairs={{0,4},{4,8},{8,12},{12,16},{16,20},{20,24},{24,28},{1,5},{5,9},{9,... | collective-permute-start | bytes 589832 | tf_op jit(solution)/shard_map/ppermute | solution.py:17
  13.2 16.3 %collective-permute-start.4 = (bf16[1,128,768]{2,1,0:T(8,128)(2,1)S(1)}, bf16[1,128,768]{2,1,0:T(8,128)(2,1)S(1)}, u32[]{:S(2)}, u32[]{:S(2)}) collective-permute-start(bf16[1,128,768]{2,1,0:T(8,128)(2,1)S(1)} %get-tuple-element.9), channel_id=1, source_target_pairs={{4,0},{8,4},{12,8},{16,12},{20,16},{24,20},{28,24},{5,1},{9,5},{13... | collective-permute-start | bytes 589832 | tf_op jit(solution)/shard_map/ppermute | solution.py:20
  16.2 12.0 %collective-permute-start.1 = (bf16[1,64,768]{2,1,0:T(8,128)(2,1)S(1)}, bf16[1,64,768]{2,1,0:T(8,128)(2,1)S(1)}, u32[]{:S(2)}, u32[]{:S(2)}) collective-permute-start(bf16[1,64,768]{2,1,0:T(8,128)(2,1)S(1)} %get-tuple-element.12), channel_id=1, source_target_pairs={{4,0},{8,4},{12,8},{16,12},{20,16},{24,20},{28,24},{5,1},{9,5},{13... | collective-permute-start | bytes 294920 | tf_op jit(solution)/shard_map/ppermute | solution.py:20
  17.5 7.9 %copy-start = (bf16[1,512,768]{2,1,0:T(8,128)(2,1)S(1)}, bf16[1,512,768]{2,1,0:T(8,128)(2,1)}, u32[]{:S(2)}) copy-start(bf16[1,512,768]{2,1,0:T(8,128)(2,1)} %param.7) | copy-start | bytes 2359300
  17.5 7.9 %copy-start.6 = (bf16[3,768,768]{2,1,0:T(8,128)(2,1)S(1)}, bf16[3,768,768]{2,1,0:T(8,128)(2,1)}, u32[]{:S(2)}) copy-start(bf16[3,768,768]{2,1,0:T(8,128)(2,1)} %param.6) | copy-start | bytes 10616836
  17.5 8.7 %collective-permute-start = (bf16[1,64,768]{2,1,0:T(8,128)(2,1)S(1)}, bf16[1,64,768]{2,1,0:T(8,128)(2,1)S(1)}, u32[]{:S(2)}, u32[]{:S(2)}) collective-permute-start(bf16[1,64,768]{2,1,0:T(8,128)(2,1)S(1)} %get-tuple-element.13), channel_id=1, source_target_pairs={{0,4},{4,8},{8,12},{12,16},{16,20},{20,24},{24,28},{1,5},{5,9},{9,... | collective-permute-start | bytes 294920 | tf_op jit(solution)/shard_map/ppermute | solution.py:17
  25.4 2.0 copy-start.7
  29.5 0.9 copy-start.4
  37.9 7.2 %copy-start.5 = (bf16[1,512,768]{2,1,0:T(8,128)(2,1)S(1)}, bf16[1,512,768]{2,1,0:T(8,128)(2,1)}, u32[]{:S(2)}) copy-start(bf16[1,512,768]{2,1,0:T(8,128)(2,1)} %copy-done.4) | copy-start | bytes 2359300
  37.9 267.3 %reduce-scatter.5.cloned.1.call-start = ((), (), s32[]{:S(2)}) async-start(), calls=%async_computation.3 | async-start | bytes 7962624 | tf_op jit(solution)/shard_map/reduce_scatter | solution.py:93
  38.0 8.7 %collective-permute-start.3 = (bf16[1,128,768]{2,1,0:T(8,128)(2,1)S(1)}, bf16[1,128,768]{2,1,0:T(8,128)(2,1)S(1)}, u32[]{:S(2)}, u32[]{:S(2)}) collective-permute-start(bf16[1,128,768]{2,1,0:T(8,128)(2,1)S(1)} %get-tuple-element.10), channel_id=1, source_target_pairs={{4,0},{8,4},{12,8},{16,12},{20,16},{24,20},{28,24},{5,1},{9,5},{13... | collective-permute-start | bytes 589832 | tf_op jit(solution)/shard_map/ppermute | solution.py:20
  39.4 15.8 %collective-permute-start.2 = (bf16[1,128,768]{2,1,0:T(8,128)(2,1)S(1)}, bf16[1,128,768]{2,1,0:T(8,128)(2,1)S(1)}, u32[]{:S(2)}, u32[]{:S(2)}) collective-permute-start(bf16[1,128,768]{2,1,0:T(8,128)(2,1)S(1)} %get-tuple-element.11), channel_id=1, source_target_pairs={{0,4},{4,8},{8,12},{12,16},{16,20},{20,24},{24,28},{1,5},{5,9},{9,... | collective-permute-start | bytes 589832 | tf_op jit(solution)/shard_map/ppermute | solution.py:17
  59.3 293.7 %all-reduce.3.cloned.1.call-start = ((), (), s32[]{:S(2)}) async-start(), calls=%async_computation.4 | async-start | bytes 3538944 | tf_op jit(solution)/shard_map/psum | solution.py:94
  62.6 248.4 %collective-permute-start.7 = (bf16[1,64,768]{2,1,0:T(8,128)(2,1)}, bf16[1,64,768]{2,1,0:T(8,128)(2,1)}, u32[]{:S(2)}, u32[]{:S(2)}) collective-permute-start(bf16[1,64,768]{2,1,0:T(8,128)(2,1)} %get-tuple-element.6), channel_id=1, source_target_pairs={{0,4},{4,8},{8,12},{12,16},{16,20},{20,24},{24,28},{1,5},{5,9},{9,... | collective-permute-start | bytes 294920 | tf_op jit(solution)/shard_map/ppermute | solution.py:17
  67.7 241.5 %collective-permute-start.6 = (bf16[1,64,768]{2,1,0:T(8,128)(2,1)}, bf16[1,64,768]{2,1,0:T(8,128)(2,1)}, u32[]{:S(2)}, u32[]{:S(2)}) collective-permute-start(bf16[1,64,768]{2,1,0:T(8,128)(2,1)} %get-tuple-element.7), channel_id=1, source_target_pairs={{4,0},{8,4},{12,8},{16,12},{20,16},{24,20},{28,24},{5,1},{9,5},{13... | collective-permute-start | bytes 294920 | tf_op jit(solution)/shard_map/ppermute | solution.py:20
  305.3 3.9 %copy-start.8 = (bf16[3,768,768]{2,1,0:T(8,128)(2,1)S(1)}, bf16[3,768,768]{2,1,0:T(8,128)(2,1)}, u32[]{:S(2)}) copy-start(bf16[3,768,768]{2,1,0:T(8,128)(2,1)} %param.5) | copy-start | bytes 10616836
  309.1 1.9 copy-start.3
  309.1 1.9 copy-start.9
  353.0 2.2 copy-start.1
Sparse Core Ops, SparseCore 0:
  38.0 134.8 reduce-scatter.2
  177.1 128.0 reduce-scatter.4
  307.7 45.2 all-reduce.2
where the time goes:
time: 363 us
  waiting for transfers between devices  277 us (76%)
  matrix products  31.5 us (9%)
  starting transfers between devices  26.4 us (7%)
  between operations  14.1 us (4%)
  other arithmetic  7.92 us (2%)
  local copies, waits for them, and re-layouts  6.22 us (2%)
    reduce_scatter x2, waiting for transfers between devices, kernel_reduction(): share = lax.psum_scatter(terms, 'seq', scatter_dimension=1, tiled=True)  230 us
    psum x1, waiting for transfers between devices, kernel_reduction(): return lax.psum(share, 'dp')  38.4 us
    ppermute x4, starting transfers between devices, padded(): lax.ppermute(lax.slice_in_dim(block, block.shape[dim] - width, None, axis...  21 us
    dot_general x4, matrix products, convolve_forward(): jnp.einsum('wlc,cd->wld', padded_input[:, tap_index * dilation_step:tap_i...  10.1 us
    dot_general x4, matrix products, convolve_backward(): jnp.einsum('wld,cd->wlc', gradient_padded[:, (2 - tap_index) * dilation_s...  9.38 us
    ppermute x4, waiting for transfers between devices, padded(): lax.ppermute(lax.slice_in_dim(block, block.shape[dim] - width, None, axis...  7.76 us
  transfers between devices with their start and end apart: 11, of which 5 were waited for; matrix products, arithmetic and copies ran while one was open for 9% of the time, Pallas kernels for 0%

commit v1 on v0

--- a/solution.py
+++ b/solution.py
@@ -1,8 +1,11 @@
+import functools
 import math
 
 import jax
 import jax.numpy as jnp
 from jax import lax
+from jax.experimental import pallas as pl
+from jax.experimental.pallas import tpu as pltpu
 from jax.sharding import PartitionSpec as P
 
 FIRST_DILATION = 64
@@ -92,6 +95,159 @@
 def kernel_reduction(terms):
     share = lax.psum_scatter(terms, "seq", scatter_dimension=1, tiled=True)
     return lax.psum(share, "dp")
+
+
+AXES = ("z1", "z0", "x")
+ORDERS = (("x", "y", "z0", "z1"), ("y", "x", "z0", "z1"), ("z0", "z1", "x", "y"))
+STEPS = 7
+
+
+def landing_shapes(order, rows, columns):
+    free, width = list(AXES), columns
+    shapes = [(2,) * len(free) + (rows, width)]
+    for axis in order:
+        if axis == "y":
+            width //= 2
+        else:
+            free.remove(axis)
+        shapes.append((2,) * len(free) + (rows, width))
+    return shapes
+
+
+def reduce_kernel(scale, count, dilations, *refs):
+    a_pad, a_grad, b_pad, b_grad, out_a, out_b = refs[:6]
+    total, part, gathered = refs[6:9]
+    landings = refs[9:-2]
+    send_sem, recv_sem = refs[-2:]
+    seq, dp = lax.axis_index("seq"), lax.axis_index("dp")
+    mine = {
+        "core": dp % 2,
+        "y": dp // 2,
+        "x": seq % 2,
+        "z0": (seq // 2) % 2,
+        "z1": seq // 4,
+    }
+    stride = {"x": 1, "z0": 2, "z1": 4}
+    partner = {
+        "core": {"seq": seq, "dp": dp + 1 - 2 * mine["core"]},
+        "y": {"seq": seq, "dp": dp + 2 - 4 * mine["y"]},
+    }
+    for axis, step in stride.items():
+        partner[axis] = {"seq": seq + step - 2 * step * mine[axis], "dp": dp}
+
+    barrier = pltpu.get_barrier_semaphore()
+    for device in partner.values():
+        pl.semaphore_signal(barrier, inc=1, device_id=device, device_id_type=pl.DeviceIdType.MESH)
+    pl.semaphore_wait(barrier, len(partner))
+
+    columns = total.shape[-1]
+    half = columns // 2
+
+    def column_slice(which):
+        return pl.ds(pl.multiple_of(which * half, half), half)
+
+    def region(tap, at):
+        index = [tap]
+        for axis in AXES:
+            index.append(at.get(axis, slice(None)))
+        index += [at["core"], slice(None)]
+        index.append(column_slice(at["y"]) if "y" in at else slice(None))
+        return tuple(index)
+
+    copies = []
+
+    def send(src, dst, tap, step, axis):
+        copy = pltpu.make_async_remote_copy(
+            src_ref=src,
+            dst_ref=dst,
+            send_sem=send_sem.at[tap, step],
+            recv_sem=recv_sem.at[tap, step],
+            device_id=partner[axis],
+            device_id_type=pl.DeviceIdType.MESH,
+        )
+        copy.start()
+        copies.append(copy)
+        return copy
+
+    waiting, at = {}, {}
+    for tap in range(6):
+        layer, offset = 1 - tap // 3, (tap % 3) * dilations[1 - tap // 3]
+        pad, grad = (a_pad, a_grad) if layer == 0 else (b_pad, b_grad)
+        rows = total.shape[5] * 8
+        for block in range(2):
+            product = lax.dot_general(
+                pad[offset : offset + count, block * rows : (block + 1) * rows],
+                grad[...],
+                (((0,), (0,)), ((), ())),
+                preferred_element_type=jnp.float32,
+            ).reshape(total.shape[2:])
+            total[tap, block] = product
+            part[tap, block] = product.astype(jnp.bfloat16)
+        at[tap] = {"core": mine["core"]}
+        waiting[tap] = send(
+            part.at[region(tap, {"core": 1 - mine["core"]})], landings[5 * tap], tap, 0, "core"
+        )
+    for step in range(1, 6):
+        for tap in range(6):
+            waiting[tap].wait_recv()
+            keep = region(tap, at[tap])
+            summed = total[keep] + landings[5 * tap + step - 1][...].astype(jnp.float32)
+            if step < 5:
+                total[keep] = summed
+                axis = ORDERS[tap % 3][step - 1]
+                away = region(tap, {**at[tap], axis: 1 - mine[axis]})
+                part[away] = total[away].astype(jnp.bfloat16)
+                waiting[tap] = send(part.at[away], landings[5 * tap + step], tap, step, axis)
+                at[tap][axis] = mine[axis]
+            else:
+                place = gathered.at[tap, mine["core"], :, column_slice(mine["y"])]
+                place[...] = summed.astype(jnp.bfloat16)
+                waiting[tap] = send(place, place, tap, step, "y")
+    for tap in range(6):
+        waiting[tap].wait_recv()
+        place = gathered.at[tap, mine["core"]]
+        waiting[tap] = send(place, place, tap, 6, "core")
+    for tap in range(6):
+        waiting[tap].wait_recv()
+        out = out_b if tap < 3 else out_a
+        out[tap % 3] = (gathered[tap].astype(jnp.float32) * scale).reshape(out.shape[1:])
+    for copy in copies:
+        copy.wait_send()
+
+
+def reduced_products(first_margin, first_grad, second_margin, second_grad, scale):
+    channels = first_margin.shape[-1]
+    share = channels // lax.axis_size("seq")
+    rows = share // 2
+    landings = []
+    for tap in range(6):
+        for shape in landing_shapes(ORDERS[tap % 3], rows, channels):
+            landings.append(pltpu.VMEM(shape, jnp.bfloat16))
+    result = jax.ShapeDtypeStruct((3, share, channels), jnp.float32)
+    return pl.pallas_call(
+        functools.partial(
+            reduce_kernel, scale, first_grad.shape[1], (FIRST_DILATION, SECOND_DILATION)
+        ),
+        out_shape=(result, result),
+        in_specs=[pl.BlockSpec(memory_space=pltpu.VMEM)] * 4,
+        out_specs=[pl.BlockSpec(memory_space=pltpu.VMEM)] * 2,
+        scratch_shapes=[
+            pltpu.VMEM((6, 2, 2, 2, 2, rows, channels), jnp.float32),
+            pltpu.VMEM((6, 2, 2, 2, 2, rows, channels), jnp.bfloat16),
+            pltpu.VMEM((6, 2, rows, channels), jnp.bfloat16),
+            *landings,
+            pltpu.SemaphoreType.DMA((6, STEPS)),
+            pltpu.SemaphoreType.DMA((6, STEPS)),
+        ],
+        compiler_params=pltpu.CompilerParams(
+            collective_id=0, has_side_effects=True, vmem_limit_bytes=56 * 1024 * 1024
+        ),
+        cost_estimate=pl.CostEstimate(
+            flops=12 * first_grad.shape[1] * channels**2,
+            bytes_accessed=8 * 1024 * 1024,
+            transcendentals=0,
+        ),
+    )(first_margin[0], first_grad[0], second_margin[0], second_grad[0])
 
 
 def per_device(signal, first_kernel, second_kernel, cotangent):
@@ -120,18 +276,24 @@
     middle_gradient = (cotangent.astype(jnp.float32) + pull_b(second_backward)[0]).astype(
         jnp.bfloat16
     )
-    second_kernel_gradient = kernel_reduction(
-        kernel_pieces(second_margin, cotangent, SECOND_DILATION, element_count, scale_factor)
-    )
     middle_padded = borders_backward(middle_gradient, FIRST_DILATION)
     first_backward = convolve_backward(middle_padded, first_kernel, FIRST_DILATION, element_count)
     _, pull_a = jax.vjp(gelu_tanh, signal_float)
     grad_signal = (middle_gradient.astype(jnp.float32) + pull_a(first_backward)[0]).astype(
         jnp.bfloat16
     )
-    first_kernel_gradient = kernel_reduction(
-        kernel_pieces(first_margin, middle_gradient, FIRST_DILATION, element_count, scale_factor)
-    )
+    fits = n_seq == 8 and lax.axis_size("dp") == 4 and signal.shape[0] == 1
+    if fits and signal.shape[2] % 256 == 0:
+        first_kernel_gradient, second_kernel_gradient = reduced_products(
+            first_margin, middle_gradient, second_margin, cotangent, scale_factor
+        )
+    else:
+        first_kernel_gradient = kernel_reduction(
+            kernel_pieces(first_margin, middle_gradient, FIRST_DILATION, element_count, scale_factor)
+        )
+        second_kernel_gradient = kernel_reduction(
+            kernel_pieces(second_margin, cotangent, SECOND_DILATION, element_count, scale_factor)
+        )
     return (output, grad_signal, first_kernel_gradient, second_kernel_gradient)
 
 

time: 363 us -> 103 us (0.28)
  waiting for transfers between devices: 277 us -> 0.02 us
  Pallas kernels: 0 us -> 50.6 us
  matrix products: 31.5 us -> 15.7 us
  between operations: 14.1 us -> 0.93 us
  other arithmetic: 7.92 us -> 3.91 us
    reduce_scatter x2 -> x0, waiting for transfers between devices: 230 us -> none  [kernel_reduction(): share = lax.psum_scatter(terms, 'seq', scatter_dimension=1, tiled=True)]
    pallas_call x0 -> x1, Pallas kernels: none -> 50.6 us  [reduced_products(): pl.pallas_call(functools.partial(reduce_kernel, scale, first_grad.shape[1...]
    psum x1 -> x0, waiting for transfers between devices: 38.4 us -> none  [kernel_reduction(): return lax.psum(share, 'dp')]
    ppermute x4, waiting for transfers between devices: 7.76 us -> 0.01 us  [padded(): lax.ppermute(lax.slice_in_dim(block, block.shape[dim] - width, None, axis...]
    mul x2 -> x0, other arithmetic: 6.24 us -> none  [kernel_pieces(): jnp.stack([jnp.einsum('wlc,wld->cd', activation_padded[:, tap_index * dil...]
    dot_general x6 -> x0, matrix products: 5.32 us -> none  [kernel_pieces(): jnp.einsum('wlc,wld->cd', activation_padded[:, tap_index * dilation_step:...]
    dot_general x4, matrix products: 10.1 us -> 6.46 us  [convolve_forward(): jnp.einsum('wlc,cd->wld', padded_input[:, tap_index * dilation_step:tap_i...]
  transfers between devices with their start and end apart: 11 -> 8, of which waited for: 5 -> 0; matrix products, arithmetic and copies ran while one was open for 9% -> 15% of each run, Pallas kernels for 0% -> 50%
where the time goes in v1:
time: 103 us; the launch traced here: 101 us
  Pallas kernels  50.6 us (49%)
  starting transfers between devices  26.5 us (26%)
  matrix products  15.7 us (15%)
  other arithmetic  3.91 us (4%)
  local copies, waits for them, and re-layouts  3.69 us (4%)
    pallas_call x1, Pallas kernels, reduced_products(): pl.pallas_call(functools.partial(reduce_kernel, scale, first_grad.shape[1...  50.6 us
    ppermute x4, starting transfers between devices, padded(): lax.ppermute(lax.slice_in_dim(block, block.shape[dim] - width, None, axis...  21.4 us
    dot_general x4, matrix products, convolve_forward(): jnp.einsum('wlc,cd->wld', padded_input[:, tap_index * dilation_step:tap_i...  6.46 us
    dot_general x4, matrix products, convolve_backward(): jnp.einsum('wld,cd->wlc', gradient_padded[:, (2 - tap_index) * dilation_s...  6.01 us
    ppermute x4, starting transfers between devices, padded(): lax.ppermute(lax.slice_in_dim(block, 0, width, axis=dim), axis, backward)  5.17 us
    unnamed x18, local copies, waits for them, and re-layouts  3.6 us
  transfers between devices with their start and end apart: 8, of which 0 were waited for; matrix products, arithmetic and copies ran while one was open for 15% of the time, Pallas kernels for 50%

profile of v1, /device:TPU:0, one launch (start us, length us, event | category | flops | bytes accessed | tf_op | source)
XLA Modules:
  0.0 101.3 jit_solution(6084275039411922336)
XLA Ops:
  0.6 0.0 copy-start.2
  0.6 0.0 copy-start.4
  0.7 1.8 %fusion.13 = bf16[1,512,768]{2,1,0:T(8,128)(2,1)S(1)} fusion(bf16[1,512,768]{2,1,0:T(8,128)(2,1)} %param.4), kind=kLoop, calls=%fused_computation.25 | loop fusion | flops 3932160 | bytes 1572864 | tf_op jit(solution)/shard_map/convert_element_type | solution.py:259
  2.5 1.3 %collective-permute-start.1 = (bf16[1,64,768]{2,1,0:T(8,128)(2,1)S(1)}, bf16[1,64,768]{2,1,0:T(8,128)(2,1)S(1)}, u32[]{:S(2)}, u32[]{:S(2)}) collective-permute-start(bf16[1,64,768]{2,1,0:T(8,128)(2,1)S(1)} %get-tuple-element.14), channel_id=1, source_target_pairs={{4,0},{8,4},{12,8},{16,12},{20,16},{24,20},{28,24},{5,1},{9,5},{13... | collective-permute-start | bytes 294920 | tf_op jit(solution)/shard_map/ppermute | solution.py:23
  3.8 5.5 %collective-permute-start = (bf16[1,64,768]{2,1,0:T(8,128)(2,1)S(1)}, bf16[1,64,768]{2,1,0:T(8,128)(2,1)S(1)}, u32[]{:S(2)}, u32[]{:S(2)}) collective-permute-start(bf16[1,64,768]{2,1,0:T(8,128)(2,1)S(1)} %get-tuple-element.15), channel_id=1, source_target_pairs={{0,4},{4,8},{8,12},{12,16},{16,20},{20,24},{24,28},{1,5},{5,9},{9,... | collective-permute-start | bytes 294920 | tf_op jit(solution)/shard_map/ppermute | solution.py:20
  9.2 0.0 copy-done.4
  9.3 1.3 %collective-permute-start.4 = (bf16[1,128,768]{2,1,0:T(8,128)(2,1)S(1)}, bf16[1,128,768]{2,1,0:T(8,128)(2,1)S(1)}, u32[]{:S(2)}, u32[]{:S(2)}) collective-permute-start(bf16[1,128,768]{2,1,0:T(8,128)(2,1)S(1)} %get-tuple-element.11), channel_id=1, source_target_pairs={{4,0},{8,4},{12,8},{16,12},{20,16},{24,20},{28,24},{5,1},{9,5},{13... | collective-permute-start | bytes 589832 | tf_op jit(solution)/shard_map/ppermute | solution.py:23
  10.6 0.0 copy-start.3
  10.6 5.7 %collective-permute-start.5 = (bf16[1,128,768]{2,1,0:T(8,128)(2,1)S(1)}, bf16[1,128,768]{2,1,0:T(8,128)(2,1)S(1)}, u32[]{:S(2)}, u32[]{:S(2)}) collective-permute-start(bf16[1,128,768]{2,1,0:T(8,128)(2,1)S(1)} %get-tuple-element.10), channel_id=1, source_target_pairs={{0,4},{4,8},{8,12},{12,16},{16,20},{20,24},{24,28},{1,5},{5,9},{9,... | collective-permute-start | bytes 589832 | tf_op jit(solution)/shard_map/ppermute | solution.py:20
  16.3 0.0 copy-done.2
  16.3 2.4 %fusion.52 = f32[512,768]{1,0:T(8,128)S(1)} fusion(bf16[3,768,768]{2,1,0:T(8,128)(2,1)} %param.5, bf16[1,512,768]{2,1,0:T(8,128)(2,1)S(1)} %copy-done.2), kind=kOutput, calls=%fused_computation.59 | convolution fusion | flops 607911936 | bytes 3538944 | tf_op jit(solution)/shard_map/wlc,cd->wld/dot_general | solution.py:40
  18.7 0.0 copy-done.3
  18.8 0.0 copy-start.7
  18.8 0.8 fusion.34
  19.6 0.0 collective-permute-done
  19.6 1.2 %copy-done.7 = bf16[3,768,768]{2,1,0:T(8,128)(2,1)S(1)} copy-done((bf16[3,768,768]{2,1,0:T(8,128)(2,1)S(1)}, bf16[3,768,768]{2,1,0:T(8,128)(2,1)}, u32[]{:S(2)}) %copy-start.7) | copy-done | bytes 3538968
  20.8 0.8 fusion.56
  21.5 0.0 collective-permute-done.1
  21.6 1.2 %fusion.20 = (bf16[1,512,768]{2,1,0:T(8,128)(2,1)S(1)}, bf16[1,512,768]{2,1,0:T(8,128)(2,1)S(1)}) fusion(bf16[3,768,768]{2,1,0:T(8,128)(2,1)S(1)} %copy-done.7, bf16[1,64,768]{2,1,0:T(8,128)(2,1)S(1)} %collective-permute-done.1, bf16[1,512,768]{2,1,0:T(8,128)(2,1)S(1)} %fusion.13, f32[512,768]{1,0:T(8,128)S(1)} %fusion.56, f32[512,768]{1,0:T(8,128)S(1)} %fusion.52, ...), kind=kOutput, calls=%fused_computation.32 | convolution fusion | flops 611450880 | bytes 7569408 | tf_op jit(solution)/shard_map/wlc,cd->wld/dot_general | solution.py:40
  22.8 4.8 %collective-permute-start.2 = (bf16[1,128,768]{2,1,0:T(8,128)(2,1)S(1)}, bf16[1,128,768]{2,1,0:T(8,128)(2,1)S(1)}, u32[]{:S(2)}, u32[]{:S(2)}) collective-permute-start(bf16[1,128,768]{2,1,0:T(8,128)(2,1)S(1)} %get-tuple-element.13), channel_id=1, source_target_pairs={{0,4},{4,8},{8,12},{12,16},{16,20},{20,24},{24,28},{1,5},{5,9},{9,... | collective-permute-start | bytes 589832 | tf_op jit(solution)/shard_map/ppermute | solution.py:20
  27.7 1.1 %fusion.36 = f32[512,768]{1,0:T(8,128)S(1)} fusion(bf16[3,768,768]{2,1,0:T(8,128)(2,1)S(1)} %copy-done.3, bf16[1,512,768]{2,1,0:T(8,128)(2,1)S(1)} %get-tuple-element.17), kind=kOutput, calls=%fused_computation.47 | convolution fusion | flops 607911936 | bytes 3538944 | tf_op jit(solution)/shard_map/wlc,cd->wld/dot_general | solution.py:40
  28.8 1.3 %collective-permute-start.3 = (bf16[1,128,768]{2,1,0:T(8,128)(2,1)S(1)}, bf16[1,128,768]{2,1,0:T(8,128)(2,1)S(1)}, u32[]{:S(2)}, u32[]{:S(2)}) collective-permute-start(bf16[1,128,768]{2,1,0:T(8,128)(2,1)S(1)} %get-tuple-element.12), channel_id=1, source_target_pairs={{4,0},{8,4},{12,8},{16,12},{20,16},{24,20},{28,24},{5,1},{9,5},{13... | collective-permute-start | bytes 589832 | tf_op jit(solution)/shard_map/ppermute | solution.py:23
  30.1 1.0 maximum_bitcast_fusion.1.refs_0_
  31.1 0.0 collective-permute-done.4
  31.1 0.8 fusion.38
  31.9 0.0 collective-permute-done.5
  31.9 1.8 %fusion.5 = bf16[1,512,768]{2,1,0:T(8,128)(2,1)S(1)} fusion(bf16[1,512,768]{2,1,0:T(8,128)(2,1)S(1)} %get-tuple-element.17, f32[512,768]{1,0:T(8,128)S(1)} %fusion.38, f32[512,768]{1,0:T(8,128)S(1)} %fusion.34, bf16[1,512,768]{2,1,0:T(8,128)(2,1)S(1)} %copy-done.4, bf16[3,768,768]{2,1,0:T(8,128)(2,1)S(1)} %copy-done.3, ...), kind=kOutput, calls=%fused_computation.17 | convolution fusion | flops 615383040 | bytes 7667712 | tf_op jit(solution)/shard_map/wld,cd->wlc/dot_general | solution.py:57
  33.7 0.0 copy-start.5
  33.7 1.3 %collective-permute-start.6 = (bf16[1,64,768]{2,1,0:T(8,128)(2,1)S(1)}, bf16[1,64,768]{2,1,0:T(8,128)(2,1)S(1)}, u32[]{:S(2)}, u32[]{:S(2)}) collective-permute-start(bf16[1,64,768]{2,1,0:T(8,128)(2,1)S(1)} %get-tuple-element.9), channel_id=1, source_target_pairs={{4,0},{8,4},{12,8},{16,12},{20,16},{24,20},{28,24},{5,1},{9,5},{13... | collective-permute-start | bytes 294920 | tf_op jit(solution)/shard_map/ppermute | solution.py:23
  35.0 5.4 %collective-permute-start.7 = (bf16[1,64,768]{2,1,0:T(8,128)(2,1)S(1)}, bf16[1,64,768]{2,1,0:T(8,128)(2,1)S(1)}, u32[]{:S(2)}, u32[]{:S(2)}) collective-permute-start(bf16[1,64,768]{2,1,0:T(8,128)(2,1)S(1)} %get-tuple-element.8), channel_id=1, source_target_pairs={{0,4},{4,8},{8,12},{12,16},{16,20},{20,24},{24,28},{1,5},{5,9},{9,... | collective-permute-start | bytes 294920 | tf_op jit(solution)/shard_map/ppermute | solution.py:20
  40.4 0.8 fusion.50
  41.2 0.0 copy-done.5
  41.2 0.0 collective-permute-done.2
  41.2 0.8 fusion.40
  42.0 0.0 collective-permute-done.3
  42.0 1.1 %maximum_bitcast_fusion.refs_2_ = bf16[768,768]{1,0:T(8,128)(2,1)} fusion(bf16[1,128,768]{2,1,0:T(8,128)(2,1)S(1)} %collective-permute-done.3, bf16[1,512,768]{2,1,0:T(8,128)(2,1)S(1)} %get-tuple-element.16, bf16[1,128,768]{2,1,0:T(8,128)(2,1)S(1)} %collective-permute-done.2), kind=kLoop, calls=%fused_computation.40 | loop fusion | flops 3538944 | bytes 2359296 | tf_op jit(solution)/shard_map/squeeze | solution.py:250
  43.1 1.7 %fusion.21 = bf16[1,512,768]{2,1,0:T(8,128)(2,1)} fusion(bf16[1,512,768]{2,1,0:T(8,128)(2,1)S(1)} %get-tuple-element.17, f32[512,768]{1,0:T(8,128)S(1)} %fusion.40, f32[512,768]{1,0:T(8,128)S(1)} %fusion.36, bf16[3,768,768]{2,1,0:T(8,128)(2,1)S(1)} %copy-done.3, bf16[1,128,768]{2,1,0:T(8,128)(2,1)S(1)} %collective-permute-done.3, ...), kind=kOutput, calls=%fused_computation.33 | convolution fusion | flops 607518720 | bytes 6881280 | tf_op jit(solution)/shard_map/wlc,cd->wld/dot_general | solution.py:40
  44.9 0.0 copy-start.6
  44.9 50.6 %shard_map.75 = (f32[3,96,768]{2,1,0:T(8,128)}, f32[3,96,768]{2,1,0:T(8,128)}) custom-call(bf16[640,768]{1,0:T(8,128)(2,1)} %maximum_bitcast_fusion.1.refs_0_, bf16[512,768]{1,0:T(8,128)(2,1)} %bitcast.105, bf16[768,768]{1,0:T(8,128)(2,1)} %maximum_bitcast_fusion.refs_2_, bf16[512,768]{1,0:T(8,128)(2,1)} %bitcast.104), custom_call_target="tpu_custom_call" | custom-call | flops 3623878656 | bytes 8388608 | tf_op jit(solution)/shard_map/pallas_call | solution.py:227
  95.4 0.0 collective-permute-done.6
  95.4 0.0 copy-done.6
  95.4 0.8 fusion.54
  96.3 0.0 copy-start.1
  96.3 0.0 collective-permute-done.7
  96.3 2.6 %fusion.9 = bf16[1,512,768]{2,1,0:T(8,128)(2,1)} fusion(bf16[1,512,768]{2,1,0:T(8,128)(2,1)S(1)} %copy-done.2, f32[512,768]{1,0:T(8,128)S(1)} %fusion.54, f32[512,768]{1,0:T(8,128)S(1)} %fusion.50, bf16[1,512,768]{2,1,0:T(8,128)(2,1)S(1)} %copy-done.6, bf16[3,768,768]{2,1,0:T(8,128)(2,1)S(1)} %copy-done.7, bf16[1,64,768]{2,1,0:T(8,128)(2,1)S(1)} %collective-permute-done.7), kind=kOutput, calls=%fused_computation.21 | convolution fusion | flops 615383040 | bytes 7569408 | tf_op jit(solution)/shard_map/wld,cd->wlc/dot_general | solution.py:57
  98.9 0.0 copy-done.1
  98.9 0.0 copy-start
  98.9 0.9 copy.10
  99.8 0.6 copy-done
  100.4 0.9 copy.11
  (4 shorter events, 0.1 us)
Async XLA Ops:
  0.6 15.7 %copy-start.2 = (bf16[1,512,768]{2,1,0:T(8,128)(2,1)S(1)}, bf16[1,512,768]{2,1,0:T(8,128)(2,1)}, u32[]{:S(2)}) copy-start(bf16[1,512,768]{2,1,0:T(8,128)(2,1)} %param.4) | copy-start | bytes 2359300
  0.6 8.6 %copy-start.4 = (bf16[1,512,768]{2,1,0:T(8,128)(2,1)S(1)}, bf16[1,512,768]{2,1,0:T(8,128)(2,1)}, u32[]{:S(2)}) copy-start(bf16[1,512,768]{2,1,0:T(8,128)(2,1)} %param.7) | copy-start | bytes 2359300
  2.5 19.1 %collective-permute-start.1 = (bf16[1,64,768]{2,1,0:T(8,128)(2,1)S(1)}, bf16[1,64,768]{2,1,0:T(8,128)(2,1)S(1)}, u32[]{:S(2)}, u32[]{:S(2)}) collective-permute-start(bf16[1,64,768]{2,1,0:T(8,128)(2,1)S(1)} %get-tuple-element.14), channel_id=1, source_target_pairs={{4,0},{8,4},{12,8},{16,12},{20,16},{24,20},{28,24},{5,1},{9,5},{13... | collective-permute-start | bytes 294920 | tf_op jit(solution)/shard_map/ppermute | solution.py:23
  3.8 15.8 %collective-permute-start = (bf16[1,64,768]{2,1,0:T(8,128)(2,1)S(1)}, bf16[1,64,768]{2,1,0:T(8,128)(2,1)S(1)}, u32[]{:S(2)}, u32[]{:S(2)}) collective-permute-start(bf16[1,64,768]{2,1,0:T(8,128)(2,1)S(1)} %get-tuple-element.15), channel_id=1, source_target_pairs={{0,4},{4,8},{8,12},{12,16},{16,20},{20,24},{24,28},{1,5},{5,9},{9,... | collective-permute-start | bytes 294920 | tf_op jit(solution)/shard_map/ppermute | solution.py:20
  9.3 21.8 %collective-permute-start.4 = (bf16[1,128,768]{2,1,0:T(8,128)(2,1)S(1)}, bf16[1,128,768]{2,1,0:T(8,128)(2,1)S(1)}, u32[]{:S(2)}, u32[]{:S(2)}) collective-permute-start(bf16[1,128,768]{2,1,0:T(8,128)(2,1)S(1)} %get-tuple-element.11), channel_id=1, source_target_pairs={{4,0},{8,4},{12,8},{16,12},{20,16},{24,20},{28,24},{5,1},{9,5},{13... | collective-permute-start | bytes 589832 | tf_op jit(solution)/shard_map/ppermute | solution.py:23
  10.6 8.1 %copy-start.3 = (bf16[3,768,768]{2,1,0:T(8,128)(2,1)S(1)}, bf16[3,768,768]{2,1,0:T(8,128)(2,1)}, u32[]{:S(2)}) copy-start(bf16[3,768,768]{2,1,0:T(8,128)(2,1)} %param.6) | copy-start | bytes 10616836
  10.6 21.3 %collective-permute-start.5 = (bf16[1,128,768]{2,1,0:T(8,128)(2,1)S(1)}, bf16[1,128,768]{2,1,0:T(8,128)(2,1)S(1)}, u32[]{:S(2)}, u32[]{:S(2)}) collective-permute-start(bf16[1,128,768]{2,1,0:T(8,128)(2,1)S(1)} %get-tuple-element.10), channel_id=1, source_target_pairs={{0,4},{4,8},{8,12},{12,16},{16,20},{20,24},{24,28},{1,5},{5,9},{9,... | collective-permute-start | bytes 589832 | tf_op jit(solution)/shard_map/ppermute | solution.py:20
  18.8 2.0 %copy-start.7 = (bf16[3,768,768]{2,1,0:T(8,128)(2,1)S(1)}, bf16[3,768,768]{2,1,0:T(8,128)(2,1)}, u32[]{:S(2)}) copy-start(bf16[3,768,768]{2,1,0:T(8,128)(2,1)} %param.5) | copy-start | bytes 10616836
  22.8 18.4 %collective-permute-start.2 = (bf16[1,128,768]{2,1,0:T(8,128)(2,1)S(1)}, bf16[1,128,768]{2,1,0:T(8,128)(2,1)S(1)}, u32[]{:S(2)}, u32[]{:S(2)}) collective-permute-start(bf16[1,128,768]{2,1,0:T(8,128)(2,1)S(1)} %get-tuple-element.13), channel_id=1, source_target_pairs={{0,4},{4,8},{8,12},{12,16},{16,20},{20,24},{24,28},{1,5},{5,9},{9,... | collective-permute-start | bytes 589832 | tf_op jit(solution)/shard_map/ppermute | solution.py:20
  28.8 13.2 %collective-permute-start.3 = (bf16[1,128,768]{2,1,0:T(8,128)(2,1)S(1)}, bf16[1,128,768]{2,1,0:T(8,128)(2,1)S(1)}, u32[]{:S(2)}, u32[]{:S(2)}) collective-permute-start(bf16[1,128,768]{2,1,0:T(8,128)(2,1)S(1)} %get-tuple-element.12), channel_id=1, source_target_pairs={{4,0},{8,4},{12,8},{16,12},{20,16},{24,20},{28,24},{5,1},{9,5},{13... | collective-permute-start | bytes 589832 | tf_op jit(solution)/shard_map/ppermute | solution.py:23
  33.7 7.5 %copy-start.5 = (bf16[1,512,768]{2,1,0:T(8,128)(2,1)}, bf16[1,512,768]{2,1,0:T(8,128)(2,1)S(1)}, u32[]{:S(2)}) copy-start(bf16[1,512,768]{2,1,0:T(8,128)(2,1)S(1)} %fusion.5) | copy-start | bytes 2359300
  33.7 61.7 %collective-permute-start.6 = (bf16[1,64,768]{2,1,0:T(8,128)(2,1)S(1)}, bf16[1,64,768]{2,1,0:T(8,128)(2,1)S(1)}, u32[]{:S(2)}, u32[]{:S(2)}) collective-permute-start(bf16[1,64,768]{2,1,0:T(8,128)(2,1)S(1)} %get-tuple-element.9), channel_id=1, source_target_pairs={{4,0},{8,4},{12,8},{16,12},{20,16},{24,20},{28,24},{5,1},{9,5},{13... | collective-permute-start | bytes 294920 | tf_op jit(solution)/shard_map/ppermute | solution.py:23
  35.0 61.2 %collective-permute-start.7 = (bf16[1,64,768]{2,1,0:T(8,128)(2,1)S(1)}, bf16[1,64,768]{2,1,0:T(8,128)(2,1)S(1)}, u32[]{:S(2)}, u32[]{:S(2)}) collective-permute-start(bf16[1,64,768]{2,1,0:T(8,128)(2,1)S(1)} %get-tuple-element.8), channel_id=1, source_target_pairs={{0,4},{4,8},{8,12},{12,16},{16,20},{20,24},{24,28},{1,5},{5,9},{9,... | collective-permute-start | bytes 294920 | tf_op jit(solution)/shard_map/ppermute | solution.py:20
  44.9 50.6 %copy-start.6 = (bf16[1,512,768]{2,1,0:T(8,128)(2,1)S(1)}, bf16[1,512,768]{2,1,0:T(8,128)(2,1)}, u32[]{:S(2)}) copy-start(bf16[1,512,768]{2,1,0:T(8,128)(2,1)} %copy-done.5) | copy-start | bytes 2359300
  96.3 2.6 %copy-start.1 = (f32[3,96,768]{2,1,0:T(8,128)S(1)}, f32[3,96,768]{2,1,0:T(8,128)}, u32[]{:S(2)}) copy-start(f32[3,96,768]{2,1,0:T(8,128)} %get-tuple-element.24) | copy-start | bytes 2654212
  98.9 1.5 %copy-start = (f32[3,96,768]{2,1,0:T(8,128)S(1)}, f32[3,96,768]{2,1,0:T(8,128)}, u32[]{:S(2)}) copy-start(f32[3,96,768]{2,1,0:T(8,128)} %get-tuple-element.25) | copy-start | bytes 2654212

commit v2 on v1

--- a/solution.py
+++ b/solution.py
@@ -12,17 +12,18 @@
 SECOND_DILATION = 128
 
 
-def padded(block, sides, width):
-    for axis, dim in sides:
-        count = lax.axis_size(axis)
-        forward = [(i, i + 1) for i in range(count - 1)]
-        backward = [(target, source) for source, target in forward]
-        low = lax.ppermute(
-            lax.slice_in_dim(block, block.shape[dim] - width, None, axis=dim), axis, forward
-        )
-        high = lax.ppermute(lax.slice_in_dim(block, 0, width, axis=dim), axis, backward)
-        block = jnp.concatenate([low, block, high], axis=dim)
-    return block
+def padded_pair(first, first_width, second, second_width):
+    count = lax.axis_size("seq")
+    forward = [(i, i + 1) for i in range(count - 1)]
+    backward = [(target, source) for source, target in forward]
+    ends = jnp.concatenate([first[:, -first_width:], second[:, -second_width:]], axis=1)
+    starts = jnp.concatenate([first[:, :first_width], second[:, :second_width]], axis=1)
+    low = lax.ppermute(ends, "seq", forward)
+    high = lax.ppermute(starts, "seq", backward)
+    return (
+        jnp.concatenate([low[:, :first_width], first, high[:, :first_width]], axis=1),
+        jnp.concatenate([low[:, first_width:], second, high[:, first_width:]], axis=1),
+    )
 
 
 def gelu_tanh(v):
@@ -82,14 +83,6 @@
         )
         * scale_factor
     )
-
-
-def borders_forward(receptive_field, dilation_step):
-    return padded(receptive_field, (("seq", 1),), dilation_step)
-
-
-def borders_backward(receptive_field, dilation_step):
-    return padded(receptive_field, (("seq", 1),), dilation_step)
 
 
 def kernel_reduction(terms):
@@ -257,26 +250,28 @@
     scale_factor = 1.0 / math.sqrt(tokens_all)
     signal_float = signal.astype(jnp.float32)
     first_activation = gelu_tanh(signal_float).astype(jnp.bfloat16)
-    first_margin = borders_forward(first_activation, FIRST_DILATION)
+    first_margin, upstream_padded = padded_pair(
+        first_activation, FIRST_DILATION, cotangent, SECOND_DILATION
+    )
     hidden_state = (
         signal_float + convolve_forward(first_margin, first_kernel, FIRST_DILATION, element_count)
     ).astype(jnp.bfloat16)
     middle_float = hidden_state.astype(jnp.float32)
     second_activation = gelu_tanh(middle_float).astype(jnp.bfloat16)
-    second_margin = borders_forward(second_activation, SECOND_DILATION)
+    second_backward = convolve_backward(
+        upstream_padded, second_kernel, SECOND_DILATION, element_count
+    )
+    _, pull_b = jax.vjp(gelu_tanh, middle_float)
+    middle_gradient = (cotangent.astype(jnp.float32) + pull_b(second_backward)[0]).astype(
+        jnp.bfloat16
+    )
+    middle_padded, second_margin = padded_pair(
+        middle_gradient, FIRST_DILATION, second_activation, SECOND_DILATION
+    )
     output = (
         middle_float
         + convolve_forward(second_margin, second_kernel, SECOND_DILATION, element_count)
     ).astype(jnp.bfloat16)
-    upstream_padded = borders_backward(cotangent, SECOND_DILATION)
-    second_backward = convolve_backward(
-        upstream_padded, second_kernel, SECOND_DILATION, element_count
-    )
-    _, pull_b = jax.vjp(gelu_tanh, middle_float)
-    middle_gradient = (cotangent.astype(jnp.float32) + pull_b(second_backward)[0]).astype(
-        jnp.bfloat16
-    )
-    middle_padded = borders_backward(middle_gradient, FIRST_DILATION)
     first_backward = convolve_backward(middle_padded, first_kernel, FIRST_DILATION, element_count)
     _, pull_a = jax.vjp(gelu_tanh, signal_float)
     grad_signal = (middle_gradient.astype(jnp.float32) + pull_a(first_backward)[0]).astype(

time: 103 us -> 110 us (1.068)
  waiting for transfers between devices: 0.02 us -> 16.1 us
  starting transfers between devices: 26.5 us -> 12.9 us
  matrix products: 15.7 us -> 20.8 us
    ppermute x8 -> x4, waiting for transfers between devices: 0.02 us -> 16.1 us  [the longest x2 16.1 us: padded_pair(): low = lax.ppermute(ends, 'seq', forward)]
    ppermute x8 -> x4, starting transfers between devices: 26.5 us -> 12.9 us  [the longest x2 10.2 us: padded_pair(): low = lax.ppermute(ends, 'seq', forward)]
    dot_general x4, matrix products: 6.01 us -> 8.58 us  [convolve_backward(): jnp.einsum('wld,cd->wlc', gradient_padded[:, (2 - tap_index) * dilation_s...]
    dot_general x4, matrix products: 6.46 us -> 7.87 us  [convolve_forward(): jnp.einsum('wlc,cd->wld', padded_input[:, tap_index * dilation_step:tap_i...]
    unnamed x18 -> x22, local copies, waits for them, and re-layouts: 3.6 us -> 2.45 us
    dot_general x2, matrix products: 1.62 us -> 2.76 us  [convolve_backward(): jnp.einsum('wld,cd->wlc', gradient_padded[:, 2 * dilation_step:2 * dilati...]
    slice x4 -> x12, local copies, waits for them, and re-layouts: 0.09 us -> 1.2 us  [the longest x2 1.08 us: padded_pair(): second[:, :second_width]]
  transfers between devices with their start and end apart: 8 -> 4, of which waited for: 0 -> 2; matrix products, arithmetic and copies ran while one was open for 15% -> 7% of each run, Pallas kernels for 50% -> 0%
where the time goes in v2:
time: 110 us; the launch traced here: 108 us
  Pallas kernels  49.8 us (45%)
  matrix products  20.8 us (19%)
  waiting for transfers between devices  16.1 us (15%)
  starting transfers between devices  12.9 us (12%)
  other arithmetic  3.95 us (4%)
  local copies, waits for them, and re-layouts  3.65 us (3%)
    pallas_call x1, Pallas kernels, reduced_products(): pl.pallas_call(functools.partial(reduce_kernel, scale, first_grad.shape[1...  49.8 us
    ppermute x2, waiting for transfers between devices, padded_pair(): low = lax.ppermute(ends, 'seq', forward)  16.1 us
    ppermute x2, starting transfers between devices, padded_pair(): low = lax.ppermute(ends, 'seq', forward)  10.2 us
    dot_general x4, matrix products, convolve_backward(): jnp.einsum('wld,cd->wlc', gradient_padded[:, (2 - tap_index) * dilation_s...  8.58 us
    dot_general x4, matrix products, convolve_forward(): jnp.einsum('wlc,cd->wld', padded_input[:, tap_index * dilation_step:tap_i...  7.87 us
    ppermute x2, starting transfers between devices, padded_pair(): high = lax.ppermute(starts, 'seq', backward)  2.76 us
    dot_general x2, matrix products, convolve_backward(): jnp.einsum('wld,cd->wlc', gradient_padded[:, 2 * dilation_step:2 * dilati...  2.76 us
    unnamed x22, local copies, waits for them, and re-layouts  2.45 us
  transfers between devices with their start and end apart: 4, of which 2 were waited for; matrix products, arithmetic and copies ran while one was open for 7% of the time, Pallas kernels for 0%

profile of v2, /device:TPU:0, one launch (start us, length us, event | category | flops | bytes accessed | tf_op | source)
XLA Modules:
  0.0 108.2 jit_solution(8324722638260203138)
XLA Ops:
  0.6 1.1 fusion.99
  1.7 0.0 copy-start.2
  1.7 1.7 %fusion.13 = bf16[1,512,768]{2,1,0:T(8,128)(2,1)S(1)} fusion(bf16[1,512,768]{2,1,0:T(8,128)(2,1)} %param.4), kind=kLoop, calls=%fused_computation.25 | loop fusion | flops 3932160 | bytes 1572864 | tf_op jit(solution)/shard_map/convert_element_type | solution.py:252
  3.5 1.3 %collective-permute-start.1 = (bf16[1,192,768]{2,1,0:T(8,128)(2,1)S(1)}, bf16[1,192,768]{2,1,0:T(8,128)(2,1)S(1)}, u32[]{:S(2)}, u32[]{:S(2)}) collective-permute-start(bf16[1,192,768]{2,1,0:T(8,128)(2,1)S(1)} %pad_maximum_fusion.9), channel_id=1, source_target_pairs={{4,0},{8,4},{12,8},{16,12},{20,16},{24,20},{28,24},{5,1},{9,5},{13... | collective-permute-start | bytes 884744 | tf_op jit(solution)/shard_map/ppermute | solution.py:22
  4.8 0.0 copy-start.3
  4.8 0.0 copy-start.4
  4.8 5.8 %collective-permute-start = (bf16[1,192,768]{2,1,0:T(8,128)(2,1)S(1)}, bf16[1,192,768]{2,1,0:T(8,128)(2,1)S(1)}, u32[]{:S(2)}, u32[]{:S(2)}) collective-permute-start(bf16[1,192,768]{2,1,0:T(8,128)(2,1)S(1)} %pad_maximum_fusion.8), channel_id=1, source_target_pairs={{0,4},{4,8},{8,12},{12,16},{16,20},{20,24},{24,28},{1,5},{5,9},{9,... | collective-permute-start | bytes 884744 | tf_op jit(solution)/shard_map/ppermute | solution.py:21
  10.6 0.0 copy-done.2
  10.6 2.4 %fusion.40 = f32[512,768]{1,0:T(8,128)S(1)} fusion(bf16[3,768,768]{2,1,0:T(8,128)(2,1)} %param.5, bf16[1,512,768]{2,1,0:T(8,128)(2,1)S(1)} %copy-done.2), kind=kOutput, calls=%fused_computation.55 | convolution fusion | flops 607911936 | bytes 3538944 | tf_op jit(solution)/shard_map/wlc,cd->wld/dot_general | solution.py:41
  13.0 0.0 copy-done.3
  13.0 0.0 copy-done.4
  13.0 0.0 copy-start.7
  13.0 0.8 fusion.30
  13.9 8.0 %collective-permute-done = bf16[1,192,768]{2,1,0:T(8,128)(2,1)S(1)} collective-permute-done((bf16[1,192,768]{2,1,0:T(8,128)(2,1)S(1)}, bf16[1,192,768]{2,1,0:T(8,128)(2,1)S(1)}, u32[]{:S(2)}, u32[]{:S(2)}) %collective-permute-start) | collective-permute-done | bytes 294944 | tf_op jit(solution)/shard_map/ppermute | solution.py:21
  21.8 0.0 copy-done.7
  21.8 0.8 fusion.44
  22.6 0.0 collective-permute-done.1
  22.6 1.3 %fusion.22 = (bf16[1,512,768]{2,1,0:T(8,128)(2,1)S(1)}, bf16[1,512,768]{2,1,0:T(8,128)(2,1)S(1)}) fusion(bf16[3,768,768]{2,1,0:T(8,128)(2,1)S(1)} %copy-done.7, bf16[1,64,768]{2,1,0:T(8,128)(2,1)S(1)} %slice.137, bf16[1,512,768]{2,1,0:T(8,128)(2,1)S(1)} %fusion.13, f32[512,768]{1,0:T(8,128)S(1)} %fusion.44, f32[512,768]{1,0:T(8,128)S(1)} %fusion.40, ...), kind=kOutput, calls=%fused_computation.34 | convolution fusion | flops 611450880 | bytes 7569408 | tf_op jit(solution)/shard_map/wlc,cd->wld/dot_general | solution.py:41
  24.0 0.8 fusion.34
  24.8 1.1 %fusion.28 = f32[512,768]{1,0:T(8,128)S(1)} fusion(bf16[3,768,768]{2,1,0:T(8,128)(2,1)S(1)} %copy-done.3, bf16[1,512,768]{2,1,0:T(8,128)(2,1)S(1)} %get-tuple-element.17), kind=kOutput, calls=%fused_computation.43 | convolution fusion | flops 607911936 | bytes 3538944 | tf_op jit(solution)/shard_map/wlc,cd->wld/dot_general | solution.py:41
  25.9 1.8 %fusion.5 = bf16[1,512,768]{2,1,0:T(8,128)(2,1)S(1)} fusion(bf16[1,512,768]{2,1,0:T(8,128)(2,1)S(1)} %get-tuple-element.17, f32[512,768]{1,0:T(8,128)S(1)} %fusion.34, f32[512,768]{1,0:T(8,128)S(1)} %fusion.30, bf16[1,512,768]{2,1,0:T(8,128)(2,1)S(1)} %copy-done.4, bf16[3,768,768]{2,1,0:T(8,128)(2,1)S(1)} %copy-done.3, bf16[1,128,768]{2,1,0:T(8,128)(2,1)S(1)} %slice.139), kind=kOutput, calls=%fused_computation.17 | convolution fusion | flops 615383040 | bytes 7667712 | tf_op jit(solution)/shard_map/wld,cd->wlc/dot_general | solution.py:58
  27.7 0.0 copy-start.5
  27.8 4.4 %collective-permute-start.2 = (bf16[1,192,768]{2,1,0:T(8,128)(2,1)S(1)}, bf16[1,192,768]{2,1,0:T(8,128)(2,1)S(1)}, u32[]{:S(2)}, u32[]{:S(2)}) collective-permute-start(bf16[1,192,768]{2,1,0:T(8,128)(2,1)S(1)} %pad_maximum_fusion.10), channel_id=1, source_target_pairs={{0,4},{4,8},{8,12},{12,16},{16,20},{20,24},{24,28},{1,5},{5,9},{9,... | collective-permute-start | bytes 884744 | tf_op jit(solution)/shard_map/ppermute | solution.py:21
  32.2 1.5 %collective-permute-start.3 = (bf16[1,192,768]{2,1,0:T(8,128)(2,1)S(1)}, bf16[1,192,768]{2,1,0:T(8,128)(2,1)S(1)}, u32[]{:S(2)}, u32[]{:S(2)}) collective-permute-start(bf16[1,192,768]{2,1,0:T(8,128)(2,1)S(1)} %pad_maximum_fusion.11), channel_id=1, source_target_pairs={{4,0},{8,4},{12,8},{16,12},{20,16},{24,20},{28,24},{5,1},{9,5},{13... | collective-permute-start | bytes 884744 | tf_op jit(solution)/shard_map/ppermute | solution.py:22
  33.7 2.0 %fusion.38 = f32[512,768]{1,0:T(8,128)} fusion(bf16[3,768,768]{2,1,0:T(8,128)(2,1)S(1)} %copy-done.7, bf16[1,512,768]{2,1,0:T(8,128)(2,1)S(1)} %fusion.5), kind=kOutput, calls=%fused_computation.53 | convolution fusion | flops 603979776 | bytes 3538944 | tf_op jit(solution)/shard_map/wld,cd->wlc/dot_general | solution.py:58
  35.7 1.0 maximum_bitcast_fusion.1.refs_0_
  36.7 8.2 %collective-permute-done.2 = bf16[1,192,768]{2,1,0:T(8,128)(2,1)S(1)} collective-permute-done((bf16[1,192,768]{2,1,0:T(8,128)(2,1)S(1)}, bf16[1,192,768]{2,1,0:T(8,128)(2,1)S(1)}, u32[]{:S(2)}, u32[]{:S(2)}) %collective-permute-start.2) | collective-permute-done | bytes 294944 | tf_op jit(solution)/shard_map/ppermute | solution.py:21
  44.9 0.8 fusion.32
  45.7 0.0 collective-permute-done.3
  45.7 0.0 copy-done.5
  45.8 2.0 %fusion.42 = f32[512,768]{1,0:T(8,128)} fusion(bf16[3,768,768]{2,1,0:T(8,128)(2,1)S(1)} %copy-done.7, bf16[1,64,768]{2,1,0:T(8,128)(2,1)S(1)} %slice.146, bf16[1,512,768]{2,1,0:T(8,128)(2,1)S(1)} %fusion.5), kind=kOutput, calls=%fused_computation.57 | convolution fusion | flops 605552640 | bytes 3637248 | tf_op jit(solution)/shard_map/wld,cd->wlc/dot_general | solution.py:51
  47.7 1.1 %maximum_bitcast_fusion.refs_2_ = bf16[768,768]{1,0:T(8,128)(2,1)} fusion(bf16[1,128,768]{2,1,0:T(8,128)(2,1)S(1)} %slice.145, bf16[1,512,768]{2,1,0:T(8,128)(2,1)S(1)} %get-tuple-element.16, bf16[1,128,768]{2,1,0:T(8,128)(2,1)S(1)} %slice.142), kind=kLoop, calls=%fused_computation.40 | loop fusion | flops 3538944 | bytes 2359296 | tf_op jit(solution)/shard_map/squeeze | solution.py:243
  48.8 49.8 %shard_map.75 = (f32[3,96,768]{2,1,0:T(8,128)}, f32[3,96,768]{2,1,0:T(8,128)}) custom-call(bf16[640,768]{1,0:T(8,128)(2,1)} %maximum_bitcast_fusion.1.refs_0_, bf16[512,768]{1,0:T(8,128)(2,1)} %bitcast.97, bf16[768,768]{1,0:T(8,128)(2,1)} %maximum_bitcast_fusion.refs_2_, bf16[512,768]{1,0:T(8,128)(2,1)} %bitcast.96), custom_call_target="tpu_custom_call" | custom-call | flops 3623878656 | bytes 8388608 | tf_op jit(solution)/shard_map/pallas_call | solution.py:220
  98.6 0.0 copy-start.6
  98.7 0.0 copy-start.8
  98.7 0.0 copy-start.9
  98.7 3.1 %fusion.23 = bf16[1,512,768]{2,1,0:T(8,128)(2,1)} fusion(bf16[1,512,768]{2,1,0:T(8,128)(2,1)S(1)} %get-tuple-element.17, f32[512,768]{1,0:T(8,128)S(1)} %fusion.32, f32[512,768]{1,0:T(8,128)S(1)} %fusion.28, bf16[3,768,768]{2,1,0:T(8,128)(2,1)} %param.6, bf16[1,128,768]{2,1,0:T(8,128)(2,1)S(1)} %slice.145, bf16[1,512,768]{2,1,0:T(8,128)(2,1)S(1)} %get-tuple-element.16), kind=kOutput, calls=%fused_computation.35 | convolution fusion | flops 607518720 | bytes 6881280 | tf_op jit(solution)/shard_map/wlc,cd->wld/dot_general | solution.py:41
  101.8 0.0 copy-done.6
  101.8 0.0 copy-done.8
  101.8 0.0 copy-done.9
  101.8 0.0 copy-start.1
  101.8 4.0 %fusion.9 = bf16[1,512,768]{2,1,0:T(8,128)(2,1)} fusion(bf16[1,512,768]{2,1,0:T(8,128)(2,1)S(1)} %copy-done.2, f32[512,768]{1,0:T(8,128)S(1)} %copy-done.9, f32[512,768]{1,0:T(8,128)S(1)} %copy-done.8, bf16[1,512,768]{2,1,0:T(8,128)(2,1)S(1)} %copy-done.6, bf16[3,768,768]{2,1,0:T(8,128)(2,1)} %param.5, bf16[1,64,768]{2,1,0:T(8,128)(2,1)S(1)} %slice.147), kind=kOutput, calls=%fused_computation.21 | convolution fusion | flops 615383040 | bytes 7569408 | tf_op jit(solution)/shard_map/wld,cd->wlc/dot_general | solution.py:58
  105.8 0.0 copy-done.1
  105.8 0.0 copy-start
  105.8 0.9 copy.10
  106.8 0.6 copy-done
  107.3 0.9 copy.11
  (15 shorter events, 0.2 us)
Async XLA Ops:
  1.7 8.9 %copy-start.2 = (bf16[1,512,768]{2,1,0:T(8,128)(2,1)S(1)}, bf16[1,512,768]{2,1,0:T(8,128)(2,1)}, u32[]{:S(2)}) copy-start(bf16[1,512,768]{2,1,0:T(8,128)(2,1)} %param.4) | copy-start | bytes 2359300
  3.5 19.1 %collective-permute-start.1 = (bf16[1,192,768]{2,1,0:T(8,128)(2,1)S(1)}, bf16[1,192,768]{2,1,0:T(8,128)(2,1)S(1)}, u32[]{:S(2)}, u32[]{:S(2)}) collective-permute-start(bf16[1,192,768]{2,1,0:T(8,128)(2,1)S(1)} %pad_maximum_fusion.9), channel_id=1, source_target_pairs={{4,0},{8,4},{12,8},{16,12},{20,16},{24,20},{28,24},{5,1},{9,5},{13... | collective-permute-start | bytes 884744 | tf_op jit(solution)/shard_map/ppermute | solution.py:22
  4.8 8.2 %copy-start.3 = (bf16[3,768,768]{2,1,0:T(8,128)(2,1)S(1)}, bf16[3,768,768]{2,1,0:T(8,128)(2,1)}, u32[]{:S(2)}) copy-start(bf16[3,768,768]{2,1,0:T(8,128)(2,1)} %param.6) | copy-start | bytes 10616836
  4.8 8.2 %copy-start.4 = (bf16[1,512,768]{2,1,0:T(8,128)(2,1)S(1)}, bf16[1,512,768]{2,1,0:T(8,128)(2,1)}, u32[]{:S(2)}) copy-start(bf16[1,512,768]{2,1,0:T(8,128)(2,1)} %param.7) | copy-start | bytes 2359300
  4.8 17.0 %collective-permute-start = (bf16[1,192,768]{2,1,0:T(8,128)(2,1)S(1)}, bf16[1,192,768]{2,1,0:T(8,128)(2,1)S(1)}, u32[]{:S(2)}, u32[]{:S(2)}) collective-permute-start(bf16[1,192,768]{2,1,0:T(8,128)(2,1)S(1)} %pad_maximum_fusion.8), channel_id=1, source_target_pairs={{0,4},{4,8},{8,12},{12,16},{16,20},{20,24},{24,28},{1,5},{5,9},{9,... | collective-permute-start | bytes 884744 | tf_op jit(solution)/shard_map/ppermute | solution.py:21
  13.0 8.8 %copy-start.7 = (bf16[3,768,768]{2,1,0:T(8,128)(2,1)S(1)}, bf16[3,768,768]{2,1,0:T(8,128)(2,1)}, u32[]{:S(2)}) copy-start(bf16[3,768,768]{2,1,0:T(8,128)(2,1)} %param.5) | copy-start | bytes 10616836
  27.7 18.1 %copy-start.5 = (bf16[1,512,768]{2,1,0:T(8,128)(2,1)}, bf16[1,512,768]{2,1,0:T(8,128)(2,1)S(1)}, u32[]{:S(2)}) copy-start(bf16[1,512,768]{2,1,0:T(8,128)(2,1)S(1)} %fusion.5) | copy-start | bytes 2359300
  27.8 17.1 %collective-permute-start.2 = (bf16[1,192,768]{2,1,0:T(8,128)(2,1)S(1)}, bf16[1,192,768]{2,1,0:T(8,128)(2,1)S(1)}, u32[]{:S(2)}, u32[]{:S(2)}) collective-permute-start(bf16[1,192,768]{2,1,0:T(8,128)(2,1)S(1)} %pad_maximum_fusion.10), channel_id=1, source_target_pairs={{0,4},{4,8},{8,12},{12,16},{16,20},{20,24},{24,28},{1,5},{5,9},{9,... | collective-permute-start | bytes 884744 | tf_op jit(solution)/shard_map/ppermute | solution.py:21
  32.2 13.5 %collective-permute-start.3 = (bf16[1,192,768]{2,1,0:T(8,128)(2,1)S(1)}, bf16[1,192,768]{2,1,0:T(8,128)(2,1)S(1)}, u32[]{:S(2)}, u32[]{:S(2)}) collective-permute-start(bf16[1,192,768]{2,1,0:T(8,128)(2,1)S(1)} %pad_maximum_fusion.11), channel_id=1, source_target_pairs={{4,0},{8,4},{12,8},{16,12},{20,16},{24,20},{28,24},{5,1},{9,5},{13... | collective-permute-start | bytes 884744 | tf_op jit(solution)/shard_map/ppermute | solution.py:22
  98.6 3.2 %copy-start.6 = (bf16[1,512,768]{2,1,0:T(8,128)(2,1)S(1)}, bf16[1,512,768]{2,1,0:T(8,128)(2,1)}, u32[]{:S(2)}) copy-start(bf16[1,512,768]{2,1,0:T(8,128)(2,1)} %copy-done.5) | copy-start | bytes 2359300
  98.7 3.2 %copy-start.8 = (f32[512,768]{1,0:T(8,128)S(1)}, f32[512,768]{1,0:T(8,128)}, u32[]{:S(2)}) copy-start(f32[512,768]{1,0:T(8,128)} %fusion.38) | copy-start | bytes 4718596
  98.7 3.2 %copy-start.9 = (f32[512,768]{1,0:T(8,128)S(1)}, f32[512,768]{1,0:T(8,128)}, u32[]{:S(2)}) copy-start(f32[512,768]{1,0:T(8,128)} %fusion.42) | copy-start | bytes 4718596
  101.8 4.0 %copy-start.1 = (f32[3,96,768]{2,1,0:T(8,128)S(1)}, f32[3,96,768]{2,1,0:T(8,128)}, u32[]{:S(2)}) copy-start(f32[3,96,768]{2,1,0:T(8,128)} %get-tuple-element.24) | copy-start | bytes 2654212
  105.8 1.5 %copy-start = (f32[3,96,768]{2,1,0:T(8,128)S(1)}, f32[3,96,768]{2,1,0:T(8,128)}, u32[]{:S(2)}) copy-start(f32[3,96,768]{2,1,0:T(8,128)} %get-tuple-element.25) | copy-start | bytes 2654212

commit v3 on v1

--- a/solution.py
+++ b/solution.py
@@ -98,7 +98,7 @@
 
 
 AXES = ("z1", "z0", "x")
-ORDERS = (("x", "y", "z0", "z1"), ("y", "x", "z0", "z1"), ("z0", "z1", "x", "y"))
+ORDERS = (("x", "y", "z0", "z1"), ("y", "x", "z0", "z1"), ("z0", "x", "y", "z1"))
 STEPS = 7
 
 
@@ -170,7 +170,8 @@
         return copy
 
     waiting, at = {}, {}
-    for tap in range(6):
+
+    def produce(tap):
         layer, offset = 1 - tap // 3, (tap % 3) * dilations[1 - tap // 3]
         pad, grad = (a_pad, a_grad) if layer == 0 else (b_pad, b_grad)
         rows = total.shape[5] * 8
@@ -187,22 +188,31 @@
         waiting[tap] = send(
             part.at[region(tap, {"core": 1 - mine["core"]})], landings[5 * tap], tap, 0, "core"
         )
-    for step in range(1, 6):
+
+    def advance(tap, step):
+        waiting[tap].wait_recv()
+        keep = region(tap, at[tap])
+        summed = total[keep] + landings[5 * tap + step - 1][...].astype(jnp.float32)
+        if step < 5:
+            total[keep] = summed
+            axis = ORDERS[tap % 3][step - 1]
+            away = region(tap, {**at[tap], axis: 1 - mine[axis]})
+            part[away] = total[away].astype(jnp.bfloat16)
+            waiting[tap] = send(part.at[away], landings[5 * tap + step], tap, step, axis)
+            at[tap][axis] = mine[axis]
+        else:
+            place = gathered.at[tap, mine["core"], :, column_slice(mine["y"])]
+            place[...] = summed.astype(jnp.bfloat16)
+            waiting[tap] = send(place, place, tap, step, "y")
+
+    for turn in range(8):
+        if turn < 6:
+            produce(turn)
+        if turn >= 2:
+            advance(turn - 2, 1)
+    for step in range(2, 6):
         for tap in range(6):
-            waiting[tap].wait_recv()
-            keep = region(tap, at[tap])
-            summed = total[keep] + landings[5 * tap + step - 1][...].astype(jnp.float32)
-            if step < 5:
-                total[keep] = summed
-                axis = ORDERS[tap % 3][step - 1]
-                away = region(tap, {**at[tap], axis: 1 - mine[axis]})
-                part[away] = total[away].astype(jnp.bfloat16)
-                waiting[tap] = send(part.at[away], landings[5 * tap + step], tap, step, axis)
-                at[tap][axis] = mine[axis]
-            else:
-                place = gathered.at[tap, mine["core"], :, column_slice(mine["y"])]
-                place[...] = summed.astype(jnp.bfloat16)
-                waiting[tap] = send(place, place, tap, step, "y")
+            advance(tap, step)
     for tap in range(6):
         waiting[tap].wait_recv()
         place = gathered.at[tap, mine["core"]]

time: 103 us -> 105 us (1.019); the launches traced: 101 us -> 105 us
  Pallas kernels: 50.6 us -> 53.9 us
    pallas_call x1, Pallas kernels: 50.6 us -> 53.9 us  [reduced_products(): pl.pallas_call(functools.partial(reduce_kernel, scale, first_grad.shape[1...]
  transfers between devices with their start and end apart: 8 -> 8, of which waited for: 0 -> 0; matrix products, arithmetic and copies ran while one was open for 15% -> 15% of each run, Pallas kernels for 50% -> 51%
where the time goes in v3:
time: 105 us
  Pallas kernels  53.9 us (51%)
  starting transfers between devices  26.5 us (25%)
  matrix products  15.7 us (15%)
  other arithmetic  3.91 us (4%)
  local copies, waits for them, and re-layouts  3.69 us (4%)
    pallas_call x1, Pallas kernels, reduced_products(): pl.pallas_call(functools.partial(reduce_kernel, scale, first_grad.shape[1...  53.9 us
    ppermute x4, starting transfers between devices, padded(): lax.ppermute(lax.slice_in_dim(block, block.shape[dim] - width, None, axis...  21.4 us
    dot_general x4, matrix products, convolve_forward(): jnp.einsum('wlc,cd->wld', padded_input[:, tap_index * dilation_step:tap_i...  6.46 us
    dot_general x4, matrix products, convolve_backward(): jnp.einsum('wld,cd->wlc', gradient_padded[:, (2 - tap_index) * dilation_s...  6.01 us
    ppermute x4, starting transfers between devices, padded(): lax.ppermute(lax.slice_in_dim(block, 0, width, axis=dim), axis, backward)  5.17 us
    unnamed x18, local copies, waits for them, and re-layouts  3.6 us
  transfers between devices with their start and end apart: 8, of which 0 were waited for; matrix products, arithmetic and copies ran while one was open for 15% of the time, Pallas kernels for 51%

profile of v3, /device:TPU:0, one launch (start us, length us, event | category | flops | bytes accessed | tf_op | source)
XLA Modules:
  0.0 104.6 jit_solution(14376773769379437847)
XLA Ops:
  0.6 0.0 copy-start.2
  0.6 0.0 copy-start.4
  0.7 1.8 %fusion.13 = bf16[1,512,768]{2,1,0:T(8,128)(2,1)S(1)} fusion(bf16[1,512,768]{2,1,0:T(8,128)(2,1)} %param.4), kind=kLoop, calls=%fused_computation.25 | loop fusion | flops 3932160 | bytes 1572864 | tf_op jit(solution)/shard_map/convert_element_type | solution.py:269
  2.5 1.3 %collective-permute-start.1 = (bf16[1,64,768]{2,1,0:T(8,128)(2,1)S(1)}, bf16[1,64,768]{2,1,0:T(8,128)(2,1)S(1)}, u32[]{:S(2)}, u32[]{:S(2)}) collective-permute-start(bf16[1,64,768]{2,1,0:T(8,128)(2,1)S(1)} %get-tuple-element.14), channel_id=1, source_target_pairs={{4,0},{8,4},{12,8},{16,12},{20,16},{24,20},{28,24},{5,1},{9,5},{13... | collective-permute-start | bytes 294920 | tf_op jit(solution)/shard_map/ppermute | solution.py:23
  3.8 5.5 %collective-permute-start = (bf16[1,64,768]{2,1,0:T(8,128)(2,1)S(1)}, bf16[1,64,768]{2,1,0:T(8,128)(2,1)S(1)}, u32[]{:S(2)}, u32[]{:S(2)}) collective-permute-start(bf16[1,64,768]{2,1,0:T(8,128)(2,1)S(1)} %get-tuple-element.15), channel_id=1, source_target_pairs={{0,4},{4,8},{8,12},{12,16},{16,20},{20,24},{24,28},{1,5},{5,9},{9,... | collective-permute-start | bytes 294920 | tf_op jit(solution)/shard_map/ppermute | solution.py:20
  9.2 0.0 copy-done.4
  9.3 1.3 %collective-permute-start.4 = (bf16[1,128,768]{2,1,0:T(8,128)(2,1)S(1)}, bf16[1,128,768]{2,1,0:T(8,128)(2,1)S(1)}, u32[]{:S(2)}, u32[]{:S(2)}) collective-permute-start(bf16[1,128,768]{2,1,0:T(8,128)(2,1)S(1)} %get-tuple-element.11), channel_id=1, source_target_pairs={{4,0},{8,4},{12,8},{16,12},{20,16},{24,20},{28,24},{5,1},{9,5},{13... | collective-permute-start | bytes 589832 | tf_op jit(solution)/shard_map/ppermute | solution.py:23
  10.6 0.0 copy-start.3
  10.6 5.7 %collective-permute-start.5 = (bf16[1,128,768]{2,1,0:T(8,128)(2,1)S(1)}, bf16[1,128,768]{2,1,0:T(8,128)(2,1)S(1)}, u32[]{:S(2)}, u32[]{:S(2)}) collective-permute-start(bf16[1,128,768]{2,1,0:T(8,128)(2,1)S(1)} %get-tuple-element.10), channel_id=1, source_target_pairs={{0,4},{4,8},{8,12},{12,16},{16,20},{20,24},{24,28},{1,5},{5,9},{9,... | collective-permute-start | bytes 589832 | tf_op jit(solution)/shard_map/ppermute | solution.py:20
  16.3 0.0 copy-done.2
  16.3 2.4 %fusion.52 = f32[512,768]{1,0:T(8,128)S(1)} fusion(bf16[3,768,768]{2,1,0:T(8,128)(2,1)} %param.5, bf16[1,512,768]{2,1,0:T(8,128)(2,1)S(1)} %copy-done.2), kind=kOutput, calls=%fused_computation.59 | convolution fusion | flops 607911936 | bytes 3538944 | tf_op jit(solution)/shard_map/wlc,cd->wld/dot_general | solution.py:40
  18.7 0.0 copy-done.3
  18.8 0.0 copy-start.7
  18.8 0.8 fusion.34
  19.6 0.0 collective-permute-done
  19.6 1.2 %copy-done.7 = bf16[3,768,768]{2,1,0:T(8,128)(2,1)S(1)} copy-done((bf16[3,768,768]{2,1,0:T(8,128)(2,1)S(1)}, bf16[3,768,768]{2,1,0:T(8,128)(2,1)}, u32[]{:S(2)}) %copy-start.7) | copy-done | bytes 3538968
  20.8 0.8 fusion.56
  21.5 0.0 collective-permute-done.1
  21.6 1.2 %fusion.20 = (bf16[1,512,768]{2,1,0:T(8,128)(2,1)S(1)}, bf16[1,512,768]{2,1,0:T(8,128)(2,1)S(1)}) fusion(bf16[3,768,768]{2,1,0:T(8,128)(2,1)S(1)} %copy-done.7, bf16[1,64,768]{2,1,0:T(8,128)(2,1)S(1)} %collective-permute-done.1, bf16[1,512,768]{2,1,0:T(8,128)(2,1)S(1)} %fusion.13, f32[512,768]{1,0:T(8,128)S(1)} %fusion.56, f32[512,768]{1,0:T(8,128)S(1)} %fusion.52, ...), kind=kOutput, calls=%fused_computation.32 | convolution fusion | flops 611450880 | bytes 7569408 | tf_op jit(solution)/shard_map/wlc,cd->wld/dot_general | solution.py:40
  22.8 4.8 %collective-permute-start.2 = (bf16[1,128,768]{2,1,0:T(8,128)(2,1)S(1)}, bf16[1,128,768]{2,1,0:T(8,128)(2,1)S(1)}, u32[]{:S(2)}, u32[]{:S(2)}) collective-permute-start(bf16[1,128,768]{2,1,0:T(8,128)(2,1)S(1)} %get-tuple-element.13), channel_id=1, source_target_pairs={{0,4},{4,8},{8,12},{12,16},{16,20},{20,24},{24,28},{1,5},{5,9},{9,... | collective-permute-start | bytes 589832 | tf_op jit(solution)/shard_map/ppermute | solution.py:20
  27.7 1.1 %fusion.36 = f32[512,768]{1,0:T(8,128)S(1)} fusion(bf16[3,768,768]{2,1,0:T(8,128)(2,1)S(1)} %copy-done.3, bf16[1,512,768]{2,1,0:T(8,128)(2,1)S(1)} %get-tuple-element.17), kind=kOutput, calls=%fused_computation.47 | convolution fusion | flops 607911936 | bytes 3538944 | tf_op jit(solution)/shard_map/wlc,cd->wld/dot_general | solution.py:40
  28.8 1.3 %collective-permute-start.3 = (bf16[1,128,768]{2,1,0:T(8,128)(2,1)S(1)}, bf16[1,128,768]{2,1,0:T(8,128)(2,1)S(1)}, u32[]{:S(2)}, u32[]{:S(2)}) collective-permute-start(bf16[1,128,768]{2,1,0:T(8,128)(2,1)S(1)} %get-tuple-element.12), channel_id=1, source_target_pairs={{4,0},{8,4},{12,8},{16,12},{20,16},{24,20},{28,24},{5,1},{9,5},{13... | collective-permute-start | bytes 589832 | tf_op jit(solution)/shard_map/ppermute | solution.py:23
  30.1 1.0 maximum_bitcast_fusion.1.refs_0_
  31.1 0.0 collective-permute-done.4
  31.1 0.8 fusion.38
  31.9 0.0 collective-permute-done.5
  31.9 1.8 %fusion.5 = bf16[1,512,768]{2,1,0:T(8,128)(2,1)S(1)} fusion(bf16[1,512,768]{2,1,0:T(8,128)(2,1)S(1)} %get-tuple-element.17, f32[512,768]{1,0:T(8,128)S(1)} %fusion.38, f32[512,768]{1,0:T(8,128)S(1)} %fusion.34, bf16[1,512,768]{2,1,0:T(8,128)(2,1)S(1)} %copy-done.4, bf16[3,768,768]{2,1,0:T(8,128)(2,1)S(1)} %copy-done.3, ...), kind=kOutput, calls=%fused_computation.17 | convolution fusion | flops 615383040 | bytes 7667712 | tf_op jit(solution)/shard_map/wld,cd->wlc/dot_general | solution.py:57
  33.7 0.0 copy-start.5
  33.7 1.3 %collective-permute-start.6 = (bf16[1,64,768]{2,1,0:T(8,128)(2,1)S(1)}, bf16[1,64,768]{2,1,0:T(8,128)(2,1)S(1)}, u32[]{:S(2)}, u32[]{:S(2)}) collective-permute-start(bf16[1,64,768]{2,1,0:T(8,128)(2,1)S(1)} %get-tuple-element.9), channel_id=1, source_target_pairs={{4,0},{8,4},{12,8},{16,12},{20,16},{24,20},{28,24},{5,1},{9,5},{13... | collective-permute-start | bytes 294920 | tf_op jit(solution)/shard_map/ppermute | solution.py:23
  35.0 5.4 %collective-permute-start.7 = (bf16[1,64,768]{2,1,0:T(8,128)(2,1)S(1)}, bf16[1,64,768]{2,1,0:T(8,128)(2,1)S(1)}, u32[]{:S(2)}, u32[]{:S(2)}) collective-permute-start(bf16[1,64,768]{2,1,0:T(8,128)(2,1)S(1)} %get-tuple-element.8), channel_id=1, source_target_pairs={{0,4},{4,8},{8,12},{12,16},{16,20},{20,24},{24,28},{1,5},{5,9},{9,... | collective-permute-start | bytes 294920 | tf_op jit(solution)/shard_map/ppermute | solution.py:20
  40.4 0.8 fusion.50
  41.2 0.0 copy-done.5
  41.2 0.0 collective-permute-done.2
  41.2 0.8 fusion.40
  42.0 0.0 collective-permute-done.3
  42.0 1.1 %maximum_bitcast_fusion.refs_2_ = bf16[768,768]{1,0:T(8,128)(2,1)} fusion(bf16[1,128,768]{2,1,0:T(8,128)(2,1)S(1)} %collective-permute-done.3, bf16[1,512,768]{2,1,0:T(8,128)(2,1)S(1)} %get-tuple-element.16, bf16[1,128,768]{2,1,0:T(8,128)(2,1)S(1)} %collective-permute-done.2), kind=kLoop, calls=%fused_computation.40 | loop fusion | flops 3538944 | bytes 2359296 | tf_op jit(solution)/shard_map/squeeze | solution.py:260
  43.1 1.7 %fusion.21 = bf16[1,512,768]{2,1,0:T(8,128)(2,1)} fusion(bf16[1,512,768]{2,1,0:T(8,128)(2,1)S(1)} %get-tuple-element.17, f32[512,768]{1,0:T(8,128)S(1)} %fusion.40, f32[512,768]{1,0:T(8,128)S(1)} %fusion.36, bf16[3,768,768]{2,1,0:T(8,128)(2,1)S(1)} %copy-done.3, bf16[1,128,768]{2,1,0:T(8,128)(2,1)S(1)} %collective-permute-done.3, ...), kind=kOutput, calls=%fused_computation.33 | convolution fusion | flops 607518720 | bytes 6881280 | tf_op jit(solution)/shard_map/wlc,cd->wld/dot_general | solution.py:40
  44.9 0.0 copy-start.6
  44.9 53.9 %shard_map.75 = (f32[3,96,768]{2,1,0:T(8,128)}, f32[3,96,768]{2,1,0:T(8,128)}) custom-call(bf16[640,768]{1,0:T(8,128)(2,1)} %maximum_bitcast_fusion.1.refs_0_, bf16[512,768]{1,0:T(8,128)(2,1)} %bitcast.105, bf16[768,768]{1,0:T(8,128)(2,1)} %maximum_bitcast_fusion.refs_2_, bf16[512,768]{1,0:T(8,128)(2,1)} %bitcast.104), custom_call_target="tpu_custom_call" | custom-call | flops 3623878656 | bytes 8388608 | tf_op jit(solution)/shard_map/pallas_call | solution.py:237
  98.7 0.0 collective-permute-done.6
  98.7 0.0 copy-done.6
  98.8 0.8 fusion.54
  99.6 0.0 copy-start.1
  99.6 0.0 collective-permute-done.7
  99.6 2.6 %fusion.9 = bf16[1,512,768]{2,1,0:T(8,128)(2,1)} fusion(bf16[1,512,768]{2,1,0:T(8,128)(2,1)S(1)} %copy-done.2, f32[512,768]{1,0:T(8,128)S(1)} %fusion.54, f32[512,768]{1,0:T(8,128)S(1)} %fusion.50, bf16[1,512,768]{2,1,0:T(8,128)(2,1)S(1)} %copy-done.6, bf16[3,768,768]{2,1,0:T(8,128)(2,1)S(1)} %copy-done.7, bf16[1,64,768]{2,1,0:T(8,128)(2,1)S(1)} %collective-permute-done.7), kind=kOutput, calls=%fused_computation.21 | convolution fusion | flops 615383040 | bytes 7569408 | tf_op jit(solution)/shard_map/wld,cd->wlc/dot_general | solution.py:57
  102.2 0.0 copy-done.1
  102.2 0.0 copy-start
  102.2 0.9 copy.10
  103.1 0.6 copy-done
  103.7 0.9 copy.11
  (4 shorter events, 0.1 us)
Async XLA Ops:
  0.6 15.7 %copy-start.2 = (bf16[1,512,768]{2,1,0:T(8,128)(2,1)S(1)}, bf16[1,512,768]{2,1,0:T(8,128)(2,1)}, u32[]{:S(2)}) copy-start(bf16[1,512,768]{2,1,0:T(8,128)(2,1)} %param.4) | copy-start | bytes 2359300
  0.6 8.6 %copy-start.4 = (bf16[1,512,768]{2,1,0:T(8,128)(2,1)S(1)}, bf16[1,512,768]{2,1,0:T(8,128)(2,1)}, u32[]{:S(2)}) copy-start(bf16[1,512,768]{2,1,0:T(8,128)(2,1)} %param.7) | copy-start | bytes 2359300
  2.5 19.1 %collective-permute-start.1 = (bf16[1,64,768]{2,1,0:T(8,128)(2,1)S(1)}, bf16[1,64,768]{2,1,0:T(8,128)(2,1)S(1)}, u32[]{:S(2)}, u32[]{:S(2)}) collective-permute-start(bf16[1,64,768]{2,1,0:T(8,128)(2,1)S(1)} %get-tuple-element.14), channel_id=1, source_target_pairs={{4,0},{8,4},{12,8},{16,12},{20,16},{24,20},{28,24},{5,1},{9,5},{13... | collective-permute-start | bytes 294920 | tf_op jit(solution)/shard_map/ppermute | solution.py:23
  3.8 15.8 %collective-permute-start = (bf16[1,64,768]{2,1,0:T(8,128)(2,1)S(1)}, bf16[1,64,768]{2,1,0:T(8,128)(2,1)S(1)}, u32[]{:S(2)}, u32[]{:S(2)}) collective-permute-start(bf16[1,64,768]{2,1,0:T(8,128)(2,1)S(1)} %get-tuple-element.15), channel_id=1, source_target_pairs={{0,4},{4,8},{8,12},{12,16},{16,20},{20,24},{24,28},{1,5},{5,9},{9,... | collective-permute-start | bytes 294920 | tf_op jit(solution)/shard_map/ppermute | solution.py:20
  9.3 21.8 %collective-permute-start.4 = (bf16[1,128,768]{2,1,0:T(8,128)(2,1)S(1)}, bf16[1,128,768]{2,1,0:T(8,128)(2,1)S(1)}, u32[]{:S(2)}, u32[]{:S(2)}) collective-permute-start(bf16[1,128,768]{2,1,0:T(8,128)(2,1)S(1)} %get-tuple-element.11), channel_id=1, source_target_pairs={{4,0},{8,4},{12,8},{16,12},{20,16},{24,20},{28,24},{5,1},{9,5},{13... | collective-permute-start | bytes 589832 | tf_op jit(solution)/shard_map/ppermute | solution.py:23
  10.6 8.1 %copy-start.3 = (bf16[3,768,768]{2,1,0:T(8,128)(2,1)S(1)}, bf16[3,768,768]{2,1,0:T(8,128)(2,1)}, u32[]{:S(2)}) copy-start(bf16[3,768,768]{2,1,0:T(8,128)(2,1)} %param.6) | copy-start | bytes 10616836
  10.6 21.3 %collective-permute-start.5 = (bf16[1,128,768]{2,1,0:T(8,128)(2,1)S(1)}, bf16[1,128,768]{2,1,0:T(8,128)(2,1)S(1)}, u32[]{:S(2)}, u32[]{:S(2)}) collective-permute-start(bf16[1,128,768]{2,1,0:T(8,128)(2,1)S(1)} %get-tuple-element.10), channel_id=1, source_target_pairs={{0,4},{4,8},{8,12},{12,16},{16,20},{20,24},{24,28},{1,5},{5,9},{9,... | collective-permute-start | bytes 589832 | tf_op jit(solution)/shard_map/ppermute | solution.py:20
  18.8 2.0 %copy-start.7 = (bf16[3,768,768]{2,1,0:T(8,128)(2,1)S(1)}, bf16[3,768,768]{2,1,0:T(8,128)(2,1)}, u32[]{:S(2)}) copy-start(bf16[3,768,768]{2,1,0:T(8,128)(2,1)} %param.5) | copy-start | bytes 10616836
  22.8 18.4 %collective-permute-start.2 = (bf16[1,128,768]{2,1,0:T(8,128)(2,1)S(1)}, bf16[1,128,768]{2,1,0:T(8,128)(2,1)S(1)}, u32[]{:S(2)}, u32[]{:S(2)}) collective-permute-start(bf16[1,128,768]{2,1,0:T(8,128)(2,1)S(1)} %get-tuple-element.13), channel_id=1, source_target_pairs={{0,4},{4,8},{8,12},{12,16},{16,20},{20,24},{24,28},{1,5},{5,9},{9,... | collective-permute-start | bytes 589832 | tf_op jit(solution)/shard_map/ppermute | solution.py:20
  28.8 13.2 %collective-permute-start.3 = (bf16[1,128,768]{2,1,0:T(8,128)(2,1)S(1)}, bf16[1,128,768]{2,1,0:T(8,128)(2,1)S(1)}, u32[]{:S(2)}, u32[]{:S(2)}) collective-permute-start(bf16[1,128,768]{2,1,0:T(8,128)(2,1)S(1)} %get-tuple-element.12), channel_id=1, source_target_pairs={{4,0},{8,4},{12,8},{16,12},{20,16},{24,20},{28,24},{5,1},{9,5},{13... | collective-permute-start | bytes 589832 | tf_op jit(solution)/shard_map/ppermute | solution.py:23
  33.7 7.5 %copy-start.5 = (bf16[1,512,768]{2,1,0:T(8,128)(2,1)}, bf16[1,512,768]{2,1,0:T(8,128)(2,1)S(1)}, u32[]{:S(2)}) copy-start(bf16[1,512,768]{2,1,0:T(8,128)(2,1)S(1)} %fusion.5) | copy-start | bytes 2359300
  33.7 65.0 %collective-permute-start.6 = (bf16[1,64,768]{2,1,0:T(8,128)(2,1)S(1)}, bf16[1,64,768]{2,1,0:T(8,128)(2,1)S(1)}, u32[]{:S(2)}, u32[]{:S(2)}) collective-permute-start(bf16[1,64,768]{2,1,0:T(8,128)(2,1)S(1)} %get-tuple-element.9), channel_id=1, source_target_pairs={{4,0},{8,4},{12,8},{16,12},{20,16},{24,20},{28,24},{5,1},{9,5},{13... | collective-permute-start | bytes 294920 | tf_op jit(solution)/shard_map/ppermute | solution.py:23
  35.0 64.6 %collective-permute-start.7 = (bf16[1,64,768]{2,1,0:T(8,128)(2,1)S(1)}, bf16[1,64,768]{2,1,0:T(8,128)(2,1)S(1)}, u32[]{:S(2)}, u32[]{:S(2)}) collective-permute-start(bf16[1,64,768]{2,1,0:T(8,128)(2,1)S(1)} %get-tuple-element.8), channel_id=1, source_target_pairs={{0,4},{4,8},{8,12},{12,16},{16,20},{20,24},{24,28},{1,5},{5,9},{9,... | collective-permute-start | bytes 294920 | tf_op jit(solution)/shard_map/ppermute | solution.py:20
  44.9 53.9 %copy-start.6 = (bf16[1,512,768]{2,1,0:T(8,128)(2,1)S(1)}, bf16[1,512,768]{2,1,0:T(8,128)(2,1)}, u32[]{:S(2)}) copy-start(bf16[1,512,768]{2,1,0:T(8,128)(2,1)} %copy-done.5) | copy-start | bytes 2359300
  99.6 2.6 %copy-start.1 = (f32[3,96,768]{2,1,0:T(8,128)S(1)}, f32[3,96,768]{2,1,0:T(8,128)}, u32[]{:S(2)}) copy-start(f32[3,96,768]{2,1,0:T(8,128)} %get-tuple-element.24) | copy-start | bytes 2654212
  102.2 1.5 %copy-start = (f32[3,96,768]{2,1,0:T(8,128)S(1)}, f32[3,96,768]{2,1,0:T(8,128)}, u32[]{:S(2)}) copy-start(f32[3,96,768]{2,1,0:T(8,128)} %get-tuple-element.25) | copy-start | bytes 2654212
